TPU v7x, 256 devices: a whole 4x4x8 slice. The times are simulated.
256 devices in a mesh: dp: 8 (over z_hi, y), expert: 32 (over z_lo, x, core).
Axes of the slice: x: 4, y: 4, z: 8 (z_hi: 2, z_lo: 4; z = z_hi * 4 + z_lo), core: 2. Of those that a mesh axis runs over, the one named last changes fastest.
Arguments:
- tokens: bfloat16 [32768, 2048], P(('dp', 'expert')), may hold values from -6 to 6
- cotangent: bfloat16 [32768, 2048], P(('dp', 'expert')), may hold values from -6 to 6
- gate_probs: float32 [32768, 2], P(('dp', 'expert')), may hold values from 0.2 to 1
- expert_ids: int32 [32768, 2], P(('dp', 'expert')), may hold values from 0 to 31, as said below
- route_slots: int32 [32768, 2], P(('dp', 'expert')), may hold values from 0 to 4, as said below
- hot_mask: int32 [32], replicated, may hold values from 0 to 1, as said below
- w_up: bfloat16 [32, 2048, 4096], P('expert', None, 'dp'), may hold values from -0.125 to 0.125
- w_down: bfloat16 [32, 4096, 2048], P('expert', 'dp'), may hold values from -0.09375 to 0.09375
Outputs:
- layer_out: bfloat16 [32768, 2048], P(('dp', 'expert'))
- grad_tokens: bfloat16 [32768, 2048], P(('dp', 'expert'))
- grad_up: bfloat16 [32, 2048, 4096], P(None, 'expert', 'dp')
- grad_down: bfloat16 [32, 2048, 4096], P(None, 'expert', 'dp')
Inputs may be any that keep to these rules, and one draw needn't show every extreme that they name: `expert_ids`: A token's two experts differ. Only first choices name the hot expert. Every device's 128 tokens (aligned blocks) name the hot expert at least 4 + 1 times. route_slots[t, c] is the rank of route (t, c) among the routes of the same device's 128 tokens (aligned blocks) to the same expert, counting all first choices in token order before all second choices, capped at 4. `hot_mask`: exactly one entry is 1.
All inputs are finite; a program needn't handle non-finite values.
Results may differ from a plain program's by a relative error of at most 0.014.
Values may be sent and summed in bfloat16 or wider, within the bound.
A program may use at most 128 MiB of HBM per device.

v0:
```python
import jax
import jax.numpy as jnp
from jax import lax
from jax.sharding import PartitionSpec as P

CAP = 2
HCAP = 4


def side_by_side(arrays, axis, dim, along):
    ends, at = ([], 0)
    for a in arrays[:-1]:
        at += a.shape[along]
        ends.append(at)
    both = jnp.concatenate(arrays, axis=along)
    return tuple(jnp.split(lax.all_gather(both, axis, axis=dim, tiled=True), ends, axis=along))


def spread(shard, axis, root):
    mine = lax.axis_index(axis) == root
    return lax.psum(jnp.where(mine, shard, jnp.zeros_like(shard)), axis)


def side_by_side_2(arrays, axis, split_dim, concat_dim, along):
    ends, at = ([], 0)
    for a in arrays[:-1]:
        at += a.shape[along]
        ends.append(at)
    both = jnp.concatenate(arrays, axis=along)
    return tuple(
        jnp.split(
            lax.all_to_all(both, axis, split_axis=split_dim, concat_axis=concat_dim, tiled=True),
            ends,
            axis=along,
        )
    )


def gelu_pair(preact):
    normal_cdf = 0.5 * (1.0 + lax.erf(preact * 0.7071067811865476))
    density = jnp.exp(-0.5 * preact * preact) * 0.3989422804014327
    return (preact * normal_cdf, normal_cdf + preact * density)


def contract_rows(left_rows, right_rows):
    return lax.dot_general(
        left_rows, right_rows, (((0,), (0,)), ((), ())), preferred_element_type=jnp.float32
    )


def contract_last(left_rows, right_rows):
    return lax.dot_general(
        left_rows, right_rows, (((1,), (1,)), ((), ())), preferred_element_type=jnp.float32
    )


def expert_rows(rows_in, rows_grad, up_part, down_part):
    preact = jnp.dot(rows_in, up_part, preferred_element_type=jnp.float32)
    gelu_value, gelu_slope = gelu_pair(preact)
    activation = gelu_value.astype(jnp.bfloat16)
    part_out = jnp.dot(activation, down_part, preferred_element_type=jnp.float32)
    d_pre = (contract_last(rows_grad, down_part) * gelu_slope).astype(jnp.bfloat16)
    part_back = contract_last(d_pre, up_part)
    return (part_out, part_back, activation, d_pre)


def pack_rows(select, tokens, routed):
    rows_in = jnp.einsum("ptc,td->pd", select, tokens, preferred_element_type=jnp.float32).astype(
        jnp.bfloat16
    )
    rows_grad = jnp.einsum(
        "ptc,tcd->pd", select, routed, preferred_element_type=jnp.float32
    ).astype(jnp.bfloat16)
    return (rows_in, rows_grad)


def on_device(tokens, cotangent, gate_probs, expert_ids, route_slots, hot_mask, w_up, w_down):
    expert_count = lax.axis_size("expert")
    data_count = lax.axis_size("dp")
    model_width = tokens.shape[1]
    up_local = w_up[0]
    down_local = w_down[0]
    hidden = up_local.shape[1]
    block_rows = model_width // expert_count
    expert_codes = jnp.arange(hot_mask.shape[0], dtype=jnp.int32)
    routed = (gate_probs[:, :, None] * cotangent[:, None, :].astype(jnp.float32)).astype(
        jnp.bfloat16
    )
    hot_route = jnp.sum(jnp.where(expert_ids[:, :, None] == expert_codes, hot_mask, 0), axis=2) > 0
    normal_keep = jnp.logical_and(jnp.logical_not(hot_route), route_slots < CAP)
    hot_keep = jnp.logical_and(hot_route, route_slots < HCAP)
    buffer_place = expert_ids * CAP + route_slots
    normal_codes = jnp.arange(expert_count * CAP, dtype=jnp.int32)[:, None, None]
    normal_sel = jnp.logical_and(buffer_place[None] == normal_codes, normal_keep[None]).astype(
        jnp.bfloat16
    )
    hot_codes = jnp.arange(HCAP, dtype=jnp.int32)[:, None, None]
    hot_sel = jnp.logical_and(route_slots[None] == hot_codes, hot_keep[None]).astype(jnp.bfloat16)
    dispatch_in, dispatch_grad = pack_rows(normal_sel, tokens, routed)
    dispatch_in = dispatch_in.reshape(expert_count, CAP, model_width)
    dispatch_grad = dispatch_grad.reshape(expert_count, CAP, model_width)
    shadow_in, shadow_grad = pack_rows(hot_sel, tokens, routed)
    hot_index = jnp.sum(hot_mask * expert_codes)
    hot_flag = hot_mask.astype(jnp.float32)
    arrived_in, arrived_grad = (
        lax.all_to_all(dispatch_in, "expert", split_axis=0, concat_axis=0, tiled=True),
        lax.all_to_all(dispatch_grad, "expert", split_axis=0, concat_axis=0, tiled=True),
    )
    gathered_in, gathered_grad, column_in, column_grad = (
        *side_by_side((arrived_in, arrived_grad), "dp", 0, 1),
        *side_by_side((shadow_in, shadow_grad), "dp", 0, 1),
    )
    up_hot, down_hot = (
        spread(up_local, "expert", hot_index),
        spread(down_local, "expert", hot_index),
    )
    flat_in = gathered_in.reshape(-1, model_width)
    flat_grad = gathered_grad.reshape(-1, model_width)
    part_out, part_back, activation, d_pre = expert_rows(flat_in, flat_grad, up_local, down_local)
    grad_in = contract_rows(flat_in, d_pre)
    grad_out = contract_rows(flat_grad, activation)
    hot_part_out, hot_part_back, hot_activation, hot_pre = expert_rows(
        column_in, column_grad, up_hot, down_hot
    )
    row_shape = (data_count * expert_count, CAP, model_width)
    summed_out, summed_back, hot_out_sum, hot_back_sum = (
        lax.psum_scatter(
            part_out.reshape(row_shape).astype(jnp.bfloat16), "dp", scatter_dimension=0, tiled=True
        ).astype(jnp.float32),
        lax.psum_scatter(
            part_back.reshape(row_shape).astype(jnp.bfloat16), "dp", scatter_dimension=0, tiled=True
        ).astype(jnp.float32),
        lax.psum_scatter(
            hot_part_out.astype(jnp.bfloat16), "dp", scatter_dimension=0, tiled=True
        ).astype(jnp.float32),
        lax.psum_scatter(
            hot_part_back.astype(jnp.bfloat16), "dp", scatter_dimension=0, tiled=True
        ).astype(jnp.float32),
    )
    return_out, return_back = (
        lax.all_to_all(
            summed_out.astype(jnp.bfloat16), "expert", split_axis=0, concat_axis=0, tiled=True
        ),
        lax.all_to_all(
            summed_back.astype(jnp.bfloat16), "expert", split_axis=0, concat_axis=0, tiled=True
        ),
    )
    hot_out = hot_out_sum.astype(jnp.bfloat16)
    hot_back = hot_back_sum.astype(jnp.bfloat16)
    column_rows = column_in.shape[0]
    width_in, width_grad = side_by_side_2(
        (
            column_in.reshape(column_rows, expert_count, block_rows),
            column_grad.reshape(column_rows, expert_count, block_rows),
        ),
        "expert",
        1,
        0,
        2,
    )
    width_in = width_in.reshape(-1, block_rows)
    width_grad = width_grad.reshape(-1, block_rows)
    piece_pre, piece_act = side_by_side((hot_pre, hot_activation), "expert", 0, 1)
    hot_in_block = contract_rows(width_in, piece_pre)
    hot_outg_block = contract_rows(width_grad, piece_act)
    return_out = return_out.reshape(-1, model_width)
    return_back = return_back.reshape(-1, model_width)
    route_out = jnp.einsum(
        "ptc,pd->tcd", normal_sel, return_out, preferred_element_type=jnp.float32
    ) + jnp.einsum("htc,hd->tcd", hot_sel, hot_out, preferred_element_type=jnp.float32)
    route_back = jnp.einsum(
        "ptc,pd->tcd", normal_sel, return_back, preferred_element_type=jnp.float32
    ) + jnp.einsum("htc,hd->tcd", hot_sel, hot_back, preferred_element_type=jnp.float32)
    layer_out = jnp.sum(gate_probs[:, :, None] * route_out, axis=1).astype(jnp.bfloat16)
    grad_tokens = jnp.sum(route_back, axis=1).astype(jnp.bfloat16)
    own_in, own_out = (
        lax.all_to_all(
            grad_in.astype(jnp.bfloat16).reshape(expert_count, block_rows, hidden),
            "expert",
            split_axis=0,
            concat_axis=0,
            tiled=True,
        ),
        lax.all_to_all(
            grad_out.astype(jnp.bfloat16).reshape(expert_count, block_rows, hidden),
            "expert",
            split_axis=0,
            concat_axis=0,
            tiled=True,
        ),
    )
    grad_up = (own_in.astype(jnp.float32) + hot_flag[:, None, None] * hot_in_block[None]).astype(
        jnp.bfloat16
    )
    grad_down = (
        own_out.astype(jnp.float32) + hot_flag[:, None, None] * hot_outg_block[None]
    ).astype(jnp.bfloat16)
    return (layer_out, grad_tokens, grad_up, grad_down)


def solution(mesh):
    placed = (
        P(("dp", "expert"), None),
        P(("dp", "expert"), None),
        P(("dp", "expert"), None),
        P(("dp", "expert"), None),
        P(("dp", "expert"), None),
        P(),
        P("expert", None, "dp"),
        P("expert", "dp", None),
    )
    return jax.shard_map(
        on_device,
        mesh=mesh,
        in_specs=placed,
        out_specs=(
            P(("dp", "expert"), None),
            P(("dp", "expert"), None),
            P(None, "expert", "dp"),
            P(None, "expert", "dp"),
        ),
        check_vma=False,
    )
```

profile of v0, /device:TPU:1, one launch (start us, length us, event | category | flops | bytes accessed | tf_op | source)
XLA Modules:
  0.0 644.5 jit_solution(9784244337750464126)
XLA Ops:
  8.0 0.8 select_reduce_fusion
  8.9 0.7 multiply_add_fusion
  10.2 1.1 convert_element_type.93
  11.4 1.0 fusion.1
  12.4 0.9 reshape.60
  13.3 10.1 %all-to-all-start.1 = ((bf16[32,2,2048]{2,1,0:T(2,128)(2,1)}), bf16[32,2,2048]{2,1,0:T(2,128)(2,1)S(1)}, u32[]{:S(2)}, u32[]{:S(2)}) async-start(bf16[32,2,2048]{2,1,0:T(2,128)(2,1)} %reshape.60), calls=%async_computation.1 | async-start | bytes 524288 | tf_op jit(solution)/shard_map/all_to_all | solution.py:107
  24.0 10.6 %all-to-all-done.1 = bf16[32,2,2048]{2,1,0:T(2,128)(2,1)S(1)} async-done(((bf16[32,2,2048]{2,1,0:T(2,128)(2,1)}), bf16[32,2,2048]{2,1,0:T(2,128)(2,1)S(1)}, u32[]{:S(2)}, u32[]{:S(2)}) %all-to-all-start.1) | async-done | bytes 262176 | tf_op jit(solution)/shard_map/all_to_all | solution.py:107
  34.6 14.7 %all_to_all.48 = bf16[32,2,2048]{2,1,0:T(2,128)(2,1)S(1)} all-to-all(bf16[32,2,2048]{2,1,0:T(2,128)(2,1)S(1)} %reshape.59), channel_id=1, replica_groups=mesh['dp'=8,'expert'=32] {'expert'}, dimensions={0} | all-to-all | bytes 524288 | tf_op jit(solution)/shard_map/all_to_all | solution.py:106
  49.3 1.3 pad_maximum_fusion
  50.7 1.1 fusion.60
  52.5 3.2 bitcast_select_fusion
  55.7 1.5 bitcast_select_fusion.1
  57.3 83.6 %all-gather.4.cloned.1.call-done = bf16[256,4,2048]{2,1,0:T(4,128)(2,1)} async-done(((bf16[32,4,2048]{2,1,0:T(4,128)(2,1)}), bf16[256,4,2048]{2,1,0:T(4,128)(2,1)}) %all-gather.4.cloned.1.call-update) | async-done | bytes 4194320 | tf_op jit(solution)/shard_map/all_gather | solution.py:16
  140.9 8.5 %fusion.58 = (bf16[256,2,2048]{2,1,0:T(2,128)(2,1)}, bf16[256,2,2048]{2,1,0:T(2,128)(2,1)}) fusion(bf16[256,4,2048]{2,1,0:T(4,128)(2,1)} %all-gather.4.cloned.1.call-done), kind=kLoop, calls=%fused_computation.91 | loop fusion | bytes 8388608 | tf_op jit(solution)/shard_map/split | solution.py:16
  149.3 4.2 reshape.61
  153.5 4.1 reshape.63
  157.6 3.7 multiply_convert_fusion.3
  161.3 1.5 fusion.14
  163.0 4.2 convolution_convert_fusion.2
  168.5 37.8 %all-gather = bf16[8,4,4096]{2,1,0:T(4,128)(2,1)S(1)} all-gather(bf16[1,4,4096]{2,1,0:T(4,128)(2,1)S(1)} %maximum_bitcast_fusion), channel_id=1, replica_groups=mesh['dp'=8,'expert'=32] {'dp'}, dimensions={0}, use_global_device_ids=true | all-gather | bytes 294912 | tf_op jit(solution)/shard_map/all_gather | solution.py:16
  207.0 0.8 copy.42
  207.8 30.5 %all-to-all-start.5 = ((bf16[32,32,128]{2,0,1:T(8,128)(2,1)}), bf16[32,32,128]{2,0,1:T(8,128)(2,1)S(1)}, u32[]{:S(2)}, u32[]{:S(2)}) async-start(bf16[32,32,128]{2,0,1:T(8,128)(2,1)} %copy.42), calls=%async_computation.7 | async-start | bytes 524288 | tf_op jit(solution)/shard_map/all_to_all | solution.py:32
  238.6 157.9 %all-reduce.7.cloned.1.call-done = (bf16[2048,512]{1,0:T(8,128)(2,1)}, bf16[512,2048]{1,0:T(8,128)(2,1)}) async-done(((bf16[2048,512]{1,0:T(8,128)(2,1)}, bf16[512,2048]{1,0:T(8,128)(2,1)}), (bf16[2048,512]{1,0:T(8,128)(2,1)}, bf16[512,2048]{1,0:T(8,128)(2,1)})) %all-reduce.7.cloned.1.call-update) | async-done | bytes 4194320 | tf_op jit(solution)/shard_map/psum | solution.py:21
  396.5 2.2 multiply_convert_fusion.4
  398.7 0.7 fusion.17
  400.1 4.2 convolution_convert_fusion.1
  404.4 7.8 %all-to-all-start.4 = ((bf16[32,64,512]{2,1,0:T(8,128)(2,1)}), bf16[32,64,512]{2,1,0:T(8,128)(2,1)S(1)}, u32[]{:S(2)}, u32[]{:S(2)}) async-start(bf16[32,64,512]{2,1,0:T(8,128)(2,1)} %bitcast.73), calls=%async_computation.6 | async-start | bytes 4194304 | tf_op jit(solution)/shard_map/all_to_all | solution.py:177
  412.3 1.0 dot_general.67
  413.2 4.4 convolution_convert_fusion.3
  417.7 4.2 convolution_convert_fusion
  421.9 70.7 %all-to-all-done.4 = bf16[32,64,512]{2,1,0:T(8,128)(2,1)S(1)} async-done(((bf16[32,64,512]{2,1,0:T(8,128)(2,1)}), bf16[32,64,512]{2,1,0:T(8,128)(2,1)S(1)}, u32[]{:S(2)}, u32[]{:S(2)}) %all-to-all-start.4) | async-done | bytes 2097184 | tf_op jit(solution)/shard_map/all_to_all | solution.py:177
  492.6 5.5 all-to-all-start.6
  499.4 3.1 convolution_convert_fusion.5
  502.5 1.1 convolution_convert_fusion.6
  503.7 1.9 copy.41
  505.6 47.8 %all-to-all-done.6 = bf16[32,64,512]{2,1,0:T(8,128)(2,1)} async-done(((bf16[32,64,512]{2,1,0:T(8,128)(2,1)}), bf16[32,64,512]{2,1,0:T(8,128)(2,1)}, u32[]{:S(2)}, u32[]{:S(2)}) %all-to-all-start.6) | async-done | bytes 2097184 | tf_op jit(solution)/shard_map/all_to_all | solution.py:184
  553.4 6.3 all-to-all-start.3
  559.7 1.6 fusion.22
  561.4 2.2 fusion.24
  563.6 1.9 copy.39
  565.5 6.3 all-to-all-done.3
  571.8 4.0 all-to-all-start.2
  575.9 5.1 add_convert_fusion
  581.6 5.6 all-to-all-done.2
  587.3 1.8 fusion.39
  589.1 43.5 %all-reduce.9.cloned.1.call-done = (bf16[32,2048]{1,0:T(8,128)(2,1)}, bf16[32,2048]{1,0:T(8,128)(2,1)}) async-done(((bf16[32,2048]{1,0:T(8,128)(2,1)}, bf16[32,2048]{1,0:T(8,128)(2,1)}), (bf16[32,2048]{1,0:T(8,128)(2,1)}, bf16[32,2048]{1,0:T(8,128)(2,1)})) %all-reduce.9.cloned.1.call-update) | async-done | bytes 262160
  632.6 2.3 fusion.10
  634.9 2.4 fusion.9
  (59 shorter events, 5.7 us)
Async XLA Ops:
  8.0 15.6 %copy-start = (bf16[128,2048]{1,0:T(8,128)(2,1)S(1)}, bf16[128,2048]{1,0:T(8,128)(2,1)}, u32[]{:S(2)}) copy-start(bf16[128,2048]{1,0:T(8,128)(2,1)} %param.8) | copy-start | bytes 1572868
  13.3 37.4 %copy-start.10 = (s32[32]{0:T(128)S(1)}, s32[32]{0:T(128)}, u32[]{:S(2)}) copy-start(s32[32]{0:T(128)} %param.13) | copy-start | bytes 388
  13.3 21.3 %all-to-all-start.1 = ((bf16[32,2,2048]{2,1,0:T(2,128)(2,1)}), bf16[32,2,2048]{2,1,0:T(2,128)(2,1)S(1)}, u32[]{:S(2)}, u32[]{:S(2)}) async-start(bf16[32,2,2048]{2,1,0:T(2,128)(2,1)} %reshape.60), calls=%async_computation.1 | async-start | bytes 524288 | tf_op jit(solution)/shard_map/all_to_all | solution.py:107
  23.5 117.4 %all-gather.4.cloned.1.call-start = ((), (), s32[]{:S(2)}) async-start(), calls=%async_computation.9 | async-start | bytes 4718592 | tf_op jit(solution)/shard_map/all_gather | solution.py:16
  50.7 345.9 %all-reduce.7.cloned.1.call-start = ((), (), s32[]{:S(2)}) async-start(), calls=%async_computation.13 | async-start | bytes 8388608 | tf_op jit(solution)/shard_map/psum | solution.py:21
  52.5 3.2 copy-start.4
  57.2 446.4 %reduce-scatter.5.cloned.1.call-start = ((), (), s32[]{:S(2)}) async-start(), calls=%async_computation.11 | async-start | bytes 2359296 | tf_op jit(solution)/shard_map/reduce_scatter | solution.py:130
  157.6 3.7 copy-start.5
  157.6 3.7 copy-start.6
  167.3 0.7 copy-start.7
  167.3 0.9 copy-start.8
  207.8 196.5 %all-to-all-start.5 = ((bf16[32,32,128]{2,0,1:T(8,128)(2,1)}), bf16[32,32,128]{2,0,1:T(8,128)(2,1)S(1)}, u32[]{:S(2)}, u32[]{:S(2)}) async-start(bf16[32,32,128]{2,0,1:T(8,128)(2,1)} %copy.42), calls=%async_computation.7 | async-start | bytes 524288 | tf_op jit(solution)/shard_map/all_to_all | solution.py:32
  238.4 321.3 %all-gather.6.cloned.1.call-start = ((), (), s32[]{:S(2)}) async-start(), calls=%async_computation.12 | async-start | bytes 2162688 | tf_op jit(solution)/shard_map/all_gather | solution.py:16
  396.5 2.2 copy-start.1
  404.4 88.2 %all-to-all-start.4 = ((bf16[32,64,512]{2,1,0:T(8,128)(2,1)}), bf16[32,64,512]{2,1,0:T(8,128)(2,1)S(1)}, u32[]{:S(2)}, u32[]{:S(2)}) async-start(bf16[32,64,512]{2,1,0:T(8,128)(2,1)} %bitcast.73), calls=%async_computation.6 | async-start | bytes 4194304 | tf_op jit(solution)/shard_map/all_to_all | solution.py:177
  412.2 151.4 %reduce-scatter.3.cloned.1.call-start = ((), (), s32[]{:S(2)}) async-start(), calls=%async_computation.10 | async-start | bytes 2359296 | tf_op jit(solution)/shard_map/reduce_scatter | solution.py:127
  492.6 5.5 copy-start.11
  492.6 60.8 %all-to-all-start.6 = ((bf16[32,64,512]{2,1,0:T(8,128)(2,1)}), bf16[32,64,512]{2,1,0:T(8,128)(2,1)}, u32[]{:S(2)}, u32[]{:S(2)}) async-start(bf16[32,64,512]{2,1,0:T(8,128)(2,1)} %bitcast.72), calls=%async_computation.8 | async-start | bytes 4194304 | tf_op jit(solution)/shard_map/all_to_all | solution.py:184
  498.1 134.5 %all-reduce.9.cloned.1.call-start = ((), (), s32[]{:S(2)}) async-start(), calls=%async_computation.14 | async-start | bytes 524288
  499.4 3.1 copy-start.2
  553.4 18.5 %all-to-all-start.3 = ((bf16[32,2,2048]{2,1,0:T(2,128)(2,1)}), bf16[32,2,2048]{2,1,0:T(2,128)(2,1)S(1)}, u32[]{:S(2)}, u32[]{:S(2)}) async-start(bf16[32,2,2048]{2,1,0:T(2,128)(2,1)} %copy.41), calls=%async_computation.5 | async-start | bytes 524288 | tf_op jit(solution)/shard_map/all_to_all | solution.py:144
  571.8 15.3 %all-to-all-start.2 = ((bf16[32,2,2048]{2,1,0:T(2,128)(2,1)}), bf16[32,2,2048]{2,1,0:T(2,128)(2,1)S(1)}, u32[]{:S(2)}, u32[]{:S(2)}) async-start(bf16[32,2,2048]{2,1,0:T(2,128)(2,1)} %copy.39), calls=%async_computation.3 | async-start | bytes 524288 | tf_op jit(solution)/shard_map/all_to_all | solution.py:141
  587.3 47.7 %copy-start.9 = (f32[128,2]{0,1:T(2,128)S(1)}, f32[128,2]{0,1:T(2,128)}, u32[]{:S(2)}) copy-start(f32[128,2]{0,1:T(2,128)} %param.10) | copy-start | bytes 3076
  632.6 2.3 copy-start.3
Sparse Core Ops, SparseCore 0:
  50.8 90.0 all-gather.3
  167.4 110.5 reduce-scatter.4
  418.2 104.2 reduce-scatter.2
  525.0 107.5 all-reduce.8
Sparse Core Ops, SparseCore 1:
  57.3 339.1 all-reduce.6
  400.2 90.1 all-gather.5
where the time goes:
time: 650 us; the launch traced here: 644 us
  waiting for transfers between devices  426 us (66%)
  starting transfers between devices  64.7 us (10%)
  blocking collectives  52.5 us (8%)
  matrix products  42 us (6%)
  local copies, waits for them, and re-layouts  25.7 us (4%)
  between operations  16.8 us (3%)
  other arithmetic  16.5 us (3%)
    psum x1, waiting for transfers between devices, spread(): return lax.psum(jnp.where(mine, shard, jnp.zeros_like(shard)), axis)  158 us
    all_gather x2, waiting for transfers between devices, side_by_side(): lax.all_gather(both, axis, axis=dim, tiled=True)  83.6 us
    all_to_all x1, waiting for transfers between devices, on_device(): lax.all_to_all(grad_in.astype(jnp.bfloat16).reshape(expert_count, block_r...  70.7 us
    all_to_all x1, waiting for transfers between devices, on_device(): lax.all_to_all(grad_out.astype(jnp.bfloat16).reshape(expert_count, block_...  47.8 us
    unnamed x7, waiting for transfers between devices  43.6 us
    all_gather x1, blocking collectives, side_by_side(): lax.all_gather(both, axis, axis=dim, tiled=True)  37.8 us
    all_to_all x1, starting transfers between devices, side_by_side_2(): lax.all_to_all(both, axis, split_axis=split_dim, concat_axis=concat_dim,...  30.5 us
    all_to_all x1, blocking collectives, on_device(): lax.all_to_all(dispatch_in, 'expert', split_axis=0, concat_axis=0, tiled=...  14.7 us
  transfers between devices with their start and end apart: 12, of which 8 were waited for; matrix products, arithmetic and copies ran while one was open for 11% of the time, Pallas kernels for 0%

commit v1 on v0

v1 whole, which is shorter than its diff:
```python
import functools

import jax
import jax.numpy as jnp
from jax import lax
from jax.experimental import pallas as pl
from jax.experimental.pallas import tpu as pltpu
from jax.sharding import PartitionSpec as P

CAP = 2
HCAP = 4
MESH = pl.DeviceIdType.MESH
BF = jnp.bfloat16
F32 = jnp.float32
ANY = pl.BlockSpec(memory_space=pl.ANY)
VM = pl.BlockSpec(memory_space=pltpu.VMEM)
SM = pl.BlockSpec(memory_space=pltpu.SMEM)
DMA = pltpu.SemaphoreType.DMA
Z_OFFSETS = (0, 1, 7, 2, 6, 3, 5, 4)
LIMIT = 60 * 1024 * 1024


def sds(shape, dtype=BF):
    return jax.ShapeDtypeStruct(shape, dtype)


def iota(shape, dim):
    return lax.broadcasted_iota(jnp.int32, shape, dim)


def dot(a, b):
    return jnp.dot(a, b, preferred_element_type=F32)


def dot_nt(a, b):
    return lax.dot_general(a, b, (((1,), (1,)), ((), ())), preferred_element_type=F32)


def dot_tn(a, b):
    return lax.dot_general(a, b, (((0,), (0,)), ((), ())), preferred_element_type=F32)


def ones_where(cond):
    return jnp.where(cond, 1.0, 0.0).astype(BF)


def pack_kernel(hot_ref, tokens_ref, cot_ref, gate_ref, ids_ref, slots_ref, disp_ref, hrow_ref):
    hot = hot_ref[0]
    rows = disp_ref.shape[0]
    r = iota((rows, 128), 0)
    code = (r // 16) * CAP + (r // 4) % 2
    is_grad = (r // 8) % 2
    quarter = r % 4
    hr = iota((32, 128), 0)
    hcode = (hr // 4) % 4
    h_is_grad = hr // 16
    hquarter = hr % 4
    sel, hsel = [], []
    for c in range(2):
        ids = ids_ref[c : c + 1, :]
        slot = slots_ref[c : c + 1, :]
        is_hot = ids == hot
        place = jnp.where(jnp.logical_and(jnp.logical_not(is_hot), slot < CAP), ids * CAP + slot, -1)
        hplace = jnp.where(jnp.logical_and(is_hot, slot < HCAP), slot, -1)
        sel.append(code == place)
        hsel.append(hcode == hplace)
    cot = cot_ref[...].astype(F32)
    routed = [(gate_ref[:, c : c + 1] * cot).astype(BF) for c in range(2)]
    either = jnp.logical_or(sel[0], sel[1])
    heither = jnp.logical_or(hsel[0], hsel[1])
    out = jnp.zeros((rows, 512), F32)
    hout = jnp.zeros((32, 512), F32)
    for q in range(4):
        cols = slice(q * 512, (q + 1) * 512)
        at_q = quarter == q
        hat_q = hquarter == q
        parts = (
            (tokens_ref[:, cols], either, heither, 0),
            (routed[0][:, cols], sel[0], hsel[0], 1),
            (routed[1][:, cols], sel[1], hsel[1], 1),
        )
        for data, s, hs, kind in parts:
            m = ones_where(jnp.logical_and(jnp.logical_and(s, at_q), is_grad == kind))
            out += dot(m, data)
            hm = ones_where(jnp.logical_and(jnp.logical_and(hs, hat_q), h_is_grad == kind))
            hout += dot(hm, data)
    disp_ref[...] = out.astype(BF)
    hrow_ref[...] = hout.astype(BF)


def pack(hot_index, tokens, cotangent, gate, ids_t, slots_t):
    return pl.pallas_call(
        pack_kernel,
        out_shape=(sds((512, 512)), sds((32, 512))),
        in_specs=[SM, VM, VM, VM, VM, VM],
        out_specs=(VM, VM),
        compiler_params=pltpu.CompilerParams(vmem_limit_bytes=LIMIT),
        name="pack_rows",
    )(hot_index, tokens, cotangent, gate, ids_t, slots_t)


class Place:
    def __init__(self):
        self.dp = lax.axis_index("dp")
        self.e = lax.axis_index("expert")
        self.h = self.dp // 4
        self.y = self.dp % 4
        self.z = self.e // 8
        self.x = (self.e // 2) % 4
        self.c = self.e % 2
        self.me = self.h * 32 + self.e
        self.group = self.me // 8

    def at_y(self, y):
        return (self.h * 4 + y, self.e)

    def at_x(self, x):
        return (self.dp, self.z * 8 + x * 2 + self.c)

    def at_z(self, z):
        return (self.dp, z * 8 + self.x * 2 + self.c)

    def partner(self):
        return (self.dp, self.e + 1 - 2 * self.c)

    def at_peer(self, p):
        return ((p // 32) * 4 + self.y, p % 32)


def send(src, dst, ssem, rsem, to):
    copy = pltpu.make_async_remote_copy(
        src_ref=src, dst_ref=dst, send_sem=ssem, recv_sem=rsem, device_id=to, device_id_type=MESH
    )
    copy.start()


def local(src, dst, sem):
    pltpu.make_async_copy(src, dst, sem).start()


def wait(ref, sem):
    pltpu.make_async_copy(ref, ref, sem).wait()


def greet(at):
    barrier = pltpu.get_barrier_semaphore()

    def one(k, _):
        pl.semaphore_signal(
            barrier, inc=1, device_id=at.at_peer((at.me + k) % 64), device_id_type=MESH
        )
        return 0

    lax.fori_loop(1, 64, one, 0)
    for k in range(1, 4):
        pl.semaphore_signal(
            barrier, inc=1, device_id=at.at_y((at.y + k) % 4), device_id_type=MESH
        )
    pl.semaphore_wait(barrier, 66)


def rows(start, size):
    return pl.ds(pl.multiple_of(start, 16), size)


def first_kernel(
    flags, disp, hrow, up, down,
    buf, hbuf, uph, dnh,
    p_up, p_dn, o_up, o_dn, m_up, m_dn, r_up, r_dn, t_up, t_dn,
    disp_s, disp_r, y_s, y_r, y_f, h_s, h_r, hy_s, hy_r,
    s1_s, s1_r, s1_l, s2_s, s2_m, s2_raw, s2_acc, s3_s, s3_r, s4_s, s4_r, s4_l, s5_s, s5_r, s5_f, s6_s, s6_r,
):
    at = Place()
    y, x, z, c = at.y, at.x, at.z, at.c
    yr, yl, yo = (y + 1) % 4, (y + 3) % 4, (y + 2) % 4
    xr, xl, xo = (x + 1) % 4, (x + 3) % 4, (x + 2) % 4
    arrays = ((up, o_up, p_up, 1024), (down, o_dn, p_dn, 256))
    for i, (w, own, _, n) in enumerate(arrays):
        local(w.at[rows(c * n, n)], own, s1_l.at[i])
    greet(at)
    for i, (w, _, other, n) in enumerate(arrays):
        send(w.at[rows((1 - c) * n, n)], other, s1_s.at[i], s1_r.at[i], at.partner())

    def dispatch(k, _):
        p = (at.me + k) % 64
        send(disp.at[p % 32], buf.at[y, at.me], disp_s, disp_r.at[at.group], at.at_peer(p))
        return 0

    local(disp.at[at.e], buf.at[y, at.me], disp_r.at[at.group])
    local(hrow, hbuf.at[y, at.h], h_r.at[0])
    send(hrow, hbuf.at[y, at.h], h_s, h_r.at[1], at.at_peer((at.me + 32) % 64))
    lax.fori_loop(1, 64, dispatch, 0)

    for i, (w, own, other, n) in enumerate(arrays):
        wait(own, s1_l.at[i])
        wait(other, s1_r.at[i])
    f_own, f_other = flags[0], flags[1]
    for own, other, n in ((o_up, p_up, 1024), (o_dn, p_dn, 256)):

        def choose(k, _, own=own, other=other, n=n):
            s = rows(k * (n // 16), n // 16)
            own[s] = (own[s].astype(F32) * f_own + other[s].astype(F32) * f_other).astype(BF)
            return 0

        lax.fori_loop(0, 16, choose, 0)

    ring = ((o_up, m_up, r_up, t_up, 128), (o_dn, m_dn, r_dn, t_dn, 32))
    for i, (o, m, r, t, n) in enumerate(ring):
        send(o.at[rows(xo * 2 * n, n)], m.at[0], s2_s.at[i, 0], s2_m.at[i, 0], at.at_x(xr))
        send(o.at[rows(xo * 2 * n + n, n)], m.at[1], s2_s.at[i, 1], s2_m.at[i, 1], at.at_x(xl))
        send(o.at[rows(xr * 2 * n + n, n)], r.at[0, pl.ds(n, n)], s2_s.at[i, 2], s2_raw.at[i, 0], at.at_x(xr))
        send(o.at[rows(xl * 2 * n, n)], r.at[1, pl.ds(0, n)], s2_s.at[i, 3], s2_raw.at[i, 1], at.at_x(xl))

    groups = [(at.group + off) % 8 for off in Z_OFFSETS]

    def slab(of_y, g):
        return buf.at[of_y, pl.ds(g * 8, 8)]

    def pass_on(i):
        g = groups[i]
        wait(slab(y, g), disp_r.at[g])
        send(slab(y, g), slab(y, g), y_s, y_r.at[0, i], at.at_y(yr))
        send(slab(y, g), slab(y, g), y_s, y_r.at[1, i], at.at_y(yl))

    def forward(i):
        g = groups[i]
        wait(slab(yl, g), y_r.at[0, i])
        if i % 2 == 0:
            send(slab(yl, g), slab(yl, g), y_s, y_f.at[i], at.at_y(yr))
        wait(slab(yr, g), y_r.at[1, i])
        if i % 2 == 1:
            send(slab(yr, g), slab(yr, g), y_s, y_f.at[i], at.at_y(yl))

    for i in range(4):
        pass_on(i)

    for i, (o, m, r, t, n) in enumerate(ring):
        wait(m.at[0], s2_m.at[i, 0])
        m[0] = m[0] + o[rows(xr * 2 * n, n)]
        send(m.at[0], r.at[0, pl.ds(0, n)], s2_s.at[i, 4], s2_acc.at[i, 0], at.at_x(xr))
        wait(m.at[1], s2_m.at[i, 1])
        m[1] = m[1] + o[rows(xl * 2 * n + n, n)]
        send(m.at[1], r.at[1, pl.ds(n, n)], s2_s.at[i, 5], s2_acc.at[i, 1], at.at_x(xl))

    for i in range(4, 8):
        pass_on(i)

    wait(hbuf.at[y, at.h], h_r.at[0])
    wait(hbuf.at[y, 1 - at.h], h_r.at[1])
    for k in range(1, 4):
        send(hbuf.at[y], hbuf.at[y], hy_s, hy_r, at.at_y((y + k) % 4))

    for i, (o, m, r, t, n) in enumerate(ring):
        for side, raw, acc in ((0, pl.ds(n, n), pl.ds(0, n)), (1, pl.ds(0, n), pl.ds(n, n))):
            wait(r.at[side, raw], s2_raw.at[i, side])
            wait(r.at[side, acc], s2_acc.at[i, side])
        r[0] = r[0] + r[1] + o[rows(x * 2 * n, 2 * n)]
        w = n // 2
        for k in range(1, 4):
            zz = (z + k) % 4
            send(r.at[0, rows(zz * w, w)], t.at[k - 1], s3_s.at[i, k - 1], s3_r.at[i, k - 1], at.at_z(zz))

    for i in range(4):
        forward(i)

    full = ((uph, t_up, r_up, 64), (dnh, t_dn, r_dn, 16))
    for i, (dst, t, r, w) in enumerate(full):
        for k in range(3):
            wait(t.at[k], s3_r.at[i, k])
        t[3] = t[0] + t[1] + t[2] + r[0, rows(z * w, w)]
        place = rows(c * 16 * w + x * 4 * w + z * w, w)
        local(t.at[3], dst.at[place], s4_l.at[i])
        for k in range(1, 4):
            send(t.at[3], dst.at[place], s4_s.at[i, k - 1], s4_r.at[i, k - 1], at.at_z((z + k) % 4))

    for i in range(4, 8):
        forward(i)

    for i, (dst, t, r, w) in enumerate(full):
        wait(t.at[3], s4_l.at[i])
        for k in range(3):
            wait(t.at[3], s4_r.at[i, k])

        def half(xx, b, dst=dst, w=w):
            return dst.at[rows(c * 16 * w + xx * 4 * w + b * 2 * w, 2 * w)]

        for b in range(2):
            send(half(x, b), half(x, b), s5_s.at[i, b], s5_r.at[i, 0, b], at.at_x(xr))
            send(half(x, b), half(x, b), s5_s.at[i, 2 + b], s5_r.at[i, 1, b], at.at_x(xl))
        quarter = dst.at[rows(c * 16 * w + x * 4 * w, 4 * w)]
        send(quarter, quarter, s6_s.at[i, 0], s6_r.at[i, 0], at.partner())
    for i, (dst, t, r, w) in enumerate(full):

        def half(xx, b, dst=dst, w=w):
            return dst.at[rows(c * 16 * w + xx * 4 * w + b * 2 * w, 2 * w)]

        wait(half(xl, 0), s5_r.at[i, 0, 0])
        send(half(xl, 0), half(xl, 0), s5_s.at[i, 4], s5_f.at[i, 0], at.at_x(xr))
        wait(half(xr, 1), s5_r.at[i, 1, 1])
        send(half(xr, 1), half(xr, 1), s5_s.at[i, 5], s5_f.at[i, 1], at.at_x(xl))
    for i, (dst, t, r, w) in enumerate(full):

        def half(xx, b, dst=dst, w=w):
            return dst.at[rows(c * 16 * w + xx * 4 * w + b * 2 * w, 2 * w)]

        wait(half(xl, 1), s5_r.at[i, 0, 1])
        wait(half(xr, 0), s5_r.at[i, 1, 0])
        for k, xx in ((1, xl), (2, xr)):
            quarter = dst.at[rows(c * 16 * w + xx * 4 * w, 4 * w)]
            send(quarter, quarter, s6_s.at[i, k], s6_r.at[i, k], at.partner())
    for i, (dst, t, r, w) in enumerate(full):

        def half(xx, b, dst=dst, w=w):
            return dst.at[rows(c * 16 * w + xx * 4 * w + b * 2 * w, 2 * w)]

        wait(half(xo, 0), s5_f.at[i, 0])
        wait(half(xo, 1), s5_f.at[i, 1])
        quarter = dst.at[rows(c * 16 * w + xo * 4 * w, 4 * w)]
        send(quarter, quarter, s6_s.at[i, 3], s6_r.at[i, 3], at.partner())

    for i in range(8):
        wait(slab(yo, groups[i]), y_f.at[i])
    wait(hbuf.at[pl.ds(0, 3)], hy_r)
    for i, (w, own, other, n) in enumerate(arrays):
        wait(own, s1_s.at[i])
    wait(buf.at[0, pl.ds(0, 63)], disp_s)
    wait(buf.at[pl.ds(0, 3)], y_s)
    wait(hbuf.at[pl.ds(0, 3)], hy_s)
    wait(hbuf.at[0, 0], h_s)
    for i, (o, m, r, t, n) in enumerate(ring):
        for k in range(6):
            wait(m.at[0], s2_s.at[i, k])
        for k in range(3):
            wait(t.at[0], s3_s.at[i, k])
            wait(t.at[0], s4_s.at[i, k])
    for i, (dst, t, r, w) in enumerate(full):
        for k in range(6):
            wait(dst.at[pl.ds(0, 2 * w)], s5_s.at[i, k])
        for k in range(4):
            wait(dst.at[pl.ds(0, 4 * w)], s6_s.at[i, k])
            wait(dst.at[pl.ds(0, 4 * w)], s6_r.at[i, k])


def first_exchange(flags, disp, hrow, up, down):
    return pl.pallas_call(
        first_kernel,
        out_shape=(sds((4, 64, 16, 512)), sds((4, 2, 32, 512)), sds((2048, 512)), sds((512, 2048))),
        in_specs=[SM, ANY, ANY, ANY, ANY],
        out_specs=(ANY, ANY, ANY, ANY),
        scratch_shapes=[
            pltpu.VMEM((1024, 512), BF),
            pltpu.VMEM((256, 2048), BF),
            pltpu.VMEM((1024, 512), BF),
            pltpu.VMEM((256, 2048), BF),
            pltpu.VMEM((2, 128, 512), BF),
            pltpu.VMEM((2, 32, 2048), BF),
            pltpu.VMEM((2, 256, 512), BF),
            pltpu.VMEM((2, 64, 2048), BF),
            pltpu.VMEM((4, 64, 512), BF),
            pltpu.VMEM((4, 16, 2048), BF),
            DMA, DMA((8,)), DMA, DMA((2, 8)), DMA((8,)), DMA, DMA((2,)), DMA, DMA,
            DMA((2,)), DMA((2,)), DMA((2,)),
            DMA((2, 6)), DMA((2, 2)), DMA((2, 2)), DMA((2, 2)),
            DMA((2, 3)), DMA((2, 3)), DMA((2, 3)), DMA((2, 3)), DMA((2,)),
            DMA((2, 6)), DMA((2, 2, 2)), DMA((2, 2)), DMA((2, 4)), DMA((2, 4)),
        ],
        compiler_params=pltpu.CompilerParams(
            collective_id=1, has_side_effects=True, vmem_limit_bytes=32 * 1024 * 1024
        ),
        name="first_exchange",
    )(flags, disp, hrow, up, down)


def gelu_pair(preact):
    normal_cdf = 0.5 * (1.0 + lax.erf(preact * 0.7071067811865476))
    density = jnp.exp(-0.5 * preact * preact) * 0.3989422804014327
    return (preact * normal_cdf, normal_cdf + preact * density)


def order_matrix(src_count, slot_count):
    r = iota((256, 256), 0)
    k = iota((256, 256), 1)
    slot = r % slot_count
    src = (r // slot_count) % src_count
    q = (r // 32) % 4
    a = r // 128
    return ones_where(k == src * (8 * slot_count) + a * (4 * slot_count) + slot * 4 + q)


def expert_kernel(
    buf, up, down, hbuf, uph, dnh, gu, gd, parts, hparts, apack, wsend, xs, act_s, pre_s, ys
):
    order = order_matrix(16, 2)

    def sort_rows(b, _):
        block = dot(order, buf[rows(b * 256, 256)]).astype(BF)
        for k in range(8):
            xs[k, rows(b * 32, 32)] = block[k * 32 : (k + 1) * 32]
        return 0

    lax.fori_loop(0, 16, sort_rows, 0)

    def hidden(b, _):
        s = rows(b * 128, 128)
        preact = dot(xs[0, s], up[0:512])
        dact = dot_nt(xs[4, s], down[:, 0:512])
        for q in range(1, 4):
            preact += dot(xs[q, s], up[q * 512 : (q + 1) * 512])
            dact += dot_nt(xs[4 + q, s], down[:, q * 512 : (q + 1) * 512])
        value, slope = gelu_pair(preact)
        act_s[s] = value.astype(BF)
        pre_s[s] = (dact * slope).astype(BF)
        return 0

    lax.fori_loop(0, 4, hidden, 0)

    for q in range(4):
        cols = slice(q * 512, (q + 1) * 512)
        gu[cols, :] = dot_tn(xs[q], pre_s[...]).astype(BF)
        gd[cols, :] = dot_tn(xs[4 + q], act_s[...]).astype(BF)
        ys[q] = dot(act_s[...], down[:, cols]).astype(BF)
        ys[4 + q] = dot_nt(pre_s[...], up[cols, :]).astype(BF)

    def unsort_rows(b, _):
        block = jnp.concatenate([ys[k, rows(b * 32, 32)] for k in range(8)], axis=0)
        parts[rows(b * 256, 256)] = dot_tn(order, block).astype(BF)
        return 0

    lax.fori_loop(0, 16, unsort_rows, 0)

    horder = order_matrix(8, 4)
    hx = dot(horder, hbuf[...]).astype(BF)
    hx = [hx[k * 32 : (k + 1) * 32] for k in range(8)]
    preact = dot(hx[0], uph[0:512])
    dact = dot_nt(hx[4], dnh[:, 0:512])
    for q in range(1, 4):
        preact += dot(hx[q], uph[q * 512 : (q + 1) * 512])
        dact += dot_nt(hx[4 + q], dnh[:, q * 512 : (q + 1) * 512])
    value, slope = gelu_pair(preact)
    hact = value.astype(BF)
    hpre = (dact * slope).astype(BF)
    apack[:, 0:512] = hpre
    apack[:, 512:1024] = hact
    outs = [dot(hact, dnh[:, q * 512 : (q + 1) * 512]).astype(BF) for q in range(4)]
    backs = [dot_nt(hpre, uph[q * 512 : (q + 1) * 512, :]).astype(BF) for q in range(4)]
    hparts[...] = dot_tn(horder, jnp.concatenate(outs + backs, axis=0)).astype(BF)
    i = iota((128, 128), 0)
    j = iota((128, 128), 1)
    for odd in range(2):
        take_in = ones_where(jnp.logical_and(j < 64, i == j + 64 * odd))
        take_grad = ones_where(jnp.logical_and(j >= 64, i == j - 64 + 64 * odd))
        for b in range(16):
            q, o = b // 4, (b % 4) * 128
            block = dot(hx[q][:, o : o + 128], take_in) + dot(hx[4 + q][:, o : o + 128], take_grad)
            wsend[2 * b + odd] = block.astype(BF)


def experts(buf, up, down, hbuf, uph, dnh):
    return pl.pallas_call(
        expert_kernel,
        out_shape=(
            sds((2048, 512)), sds((2048, 512)), sds((4096, 512)), sds((256, 512)),
            sds((32, 1024)), sds((32, 32, 128)),
        ),
        in_specs=[VM] * 6,
        out_specs=(VM,) * 6,
        scratch_shapes=[
            pltpu.VMEM((8, 512, 512), BF),
            pltpu.VMEM((512, 512), BF),
            pltpu.VMEM((512, 512), BF),
            pltpu.VMEM((8, 512, 512), BF),
        ],
        compiler_params=pltpu.CompilerParams(vmem_limit_bytes=LIMIT),
        name="experts",
    )(buf, up, down, hbuf, uph, dnh)


def second_kernel(
    gu, gd, parts, hparts, apack, wsend,
    ogu, ogd, rbuf, rhot, apool, wrecv,
    m, r, ret, hr, hret,
    g_s, g_r, w_s, w_r, m_s, m_r, raw_s, raw_r, acc_s, acc_r, ret_s, ret_r,
    hp_s, hp_r, hret_s, hret_r, az_s, az_r, ax_s, ax_r, ac_s, ac_r,
):
    at = Place()
    y, x, z, c = at.y, at.x, at.z, at.c
    yr, yl, yo = (y + 1) % 4, (y + 3) % 4, (y + 2) % 4
    greet(at)

    def part(of_y, g):
        return parts.at[of_y, pl.ds(g * 8, 8)]

    for i in range(4):
        send(part(yo, i), m.at[0, i], m_s, m_r.at[0, i], at.at_y(yr))
        send(part(yo, 4 + i), m.at[1, i], m_s, m_r.at[1, i], at.at_y(yl))
    for i in range(4):
        send(part(yr, 4 + i), r.at[0, 4 + i], raw_s, raw_r.at[0, i], at.at_y(yr))
        send(part(yl, i), r.at[1, i], raw_s, raw_r.at[1, i], at.at_y(yl))
    for k in range(1, 4):
        yy = (y + k) % 4
        send(hparts.at[yy], hr.at[k - 1], hp_s, hp_r.at[k - 1], at.at_y(yy))
    local(apack, apool.at[z, x, c], az_r.at[3])
    for k in range(1, 4):
        send(apack, apool.at[z, x, c], az_s, az_r.at[k - 1], at.at_z((z + k) % 4))

    def gradients(k, _):
        e = (at.e + k) % 32
        to = (at.dp, e)
        send(gu.at[pl.ds(e * 64, 64)], ogu.at[at.e], g_s.at[0], g_r.at[0], to)
        send(gd.at[pl.ds(e * 64, 64)], ogd.at[at.e], g_s.at[1], g_r.at[1], to)
        return 0

    def widths(k, _):
        e = (at.e + k) % 32
        send(wsend.at[e], wrecv.at[at.e], w_s, w_r, (at.dp, e))
        return 0

    local(gu.at[rows(at.e * 64, 64)], ogu.at[at.e], g_r.at[0])
    local(gd.at[rows(at.e * 64, 64)], ogd.at[at.e], g_r.at[1])
    local(wsend.at[at.e], wrecv.at[at.e], w_r)
    lax.fori_loop(1, 32, gradients, 0)
    lax.fori_loop(1, 32, widths, 0)

    for i in range(4):
        wait(m.at[0, i], m_r.at[0, i])
        m[0, i] = (m[0, i].astype(F32) + parts[yr, pl.ds(i * 8, 8)].astype(F32)).astype(BF)
        send(m.at[0, i], r.at[0, i], acc_s, acc_r.at[0, i], at.at_y(yr))
        wait(m.at[1, i], m_r.at[1, i])
        m[1, i] = (m[1, i].astype(F32) + parts[yl, pl.ds(32 + i * 8, 8)].astype(F32)).astype(BF)
        send(m.at[1, i], r.at[1, 4 + i], acc_s, acc_r.at[1, i], at.at_y(yl))

    for k in range(4):
        wait(apack, az_r.at[k])
    for k in range(1, 4):
        send(apool.at[:, x, c], apool.at[:, x, c], ax_s, ax_r.at[k - 1], at.at_x((x + k) % 4))
    for k in range(3):
        wait(hr.at[k], hp_r.at[k])
    hret[...] = (
        hparts[y].astype(F32) + hr[0].astype(F32) + hr[1].astype(F32) + hr[2].astype(F32)
    ).astype(BF)
    local(hret.at[at.h], rhot.at[at.h], hret_r.at[0])
    send(hret.at[1 - at.h], rhot.at[at.h], hret_s, hret_r.at[1], at.at_peer((at.me + 32) % 64))

    for i in range(8):
        side_raw, side_acc = (1, 0) if i < 4 else (0, 1)
        wait(r.at[side_raw, i], raw_r.at[side_raw, i % 4])
        wait(r.at[side_acc, i], acc_r.at[side_acc, i % 4])
        ret[pl.ds(i * 8, 8)] = (
            parts[y, pl.ds(i * 8, 8)].astype(F32) + r[0, i].astype(F32) + r[1, i].astype(F32)
        ).astype(BF)

        def give_back(j, _, i=i):
            p = i * 8 + j

            @pl.when(p != at.me)
            def _():
                send(ret.at[p], rbuf.at[at.me], ret_s, ret_r, at.at_peer(p))

            @pl.when(p == at.me)
            def _():
                local(ret.at[p], rbuf.at[p], ret_r)

            return 0

        lax.fori_loop(0, 8, give_back, 0)

    for k in range(3):
        wait(apool.at[:, 0, 0], ax_r.at[k])
    send(apool.at[:, :, c], apool.at[:, :, c], ac_s, ac_r, at.partner())

    wait(ogu, g_r.at[0])
    wait(ogd, g_r.at[1])
    wait(wrecv, w_r)
    wait(rbuf, ret_r)
    wait(rhot.at[0], hret_r.at[0])
    wait(rhot.at[0], hret_r.at[1])
    wait(apool.at[:, :, 0], ac_r)
    wait(gu.at[pl.ds(0, 31 * 64)], g_s.at[0])
    wait(gd.at[pl.ds(0, 31 * 64)], g_s.at[1])
    wait(wsend.at[pl.ds(0, 31)], w_s)
    wait(m, m_s)
    wait(m, raw_s)
    wait(m, acc_s)
    wait(ret.at[pl.ds(0, 63)], ret_s)
    wait(hr, hp_s)
    wait(hret.at[0], hret_s)
    wait(apool.at[0, 0:3, 0], az_s)
    wait(apool.at[:, 0:3, 0], ax_s)
    wait(apool.at[:, :, 0], ac_s)


def second_exchange(gu, gd, parts, hparts, apack, wsend):
    return pl.pallas_call(
        second_kernel,
        out_shape=(
            sds((32, 64, 512)), sds((32, 64, 512)), sds((64, 16, 512)), sds((2, 32, 512)),
            sds((4, 4, 2, 32, 1024)), sds((32, 32, 128)),
        ),
        in_specs=[ANY, ANY, VM, VM, ANY, ANY],
        out_specs=(ANY,) * 6,
        scratch_shapes=[
            pltpu.VMEM((2, 4, 8, 16, 512), BF),
            pltpu.VMEM((2, 8, 8, 16, 512), BF),
            pltpu.VMEM((64, 16, 512), BF),
            pltpu.VMEM((3, 2, 32, 512), BF),
            pltpu.VMEM((2, 32, 512), BF),
            DMA((2,)), DMA((2,)), DMA, DMA, DMA, DMA((2, 4)), DMA, DMA((2, 4)), DMA, DMA((2, 4)), DMA, DMA,
            DMA, DMA((3,)), DMA, DMA((2,)), DMA, DMA((4,)), DMA, DMA((3,)), DMA, DMA,
        ],
        compiler_params=pltpu.CompilerParams(
            collective_id=2, has_side_effects=True, vmem_limit_bytes=32 * 1024 * 1024
        ),
        name="second_exchange",
    )(gu, gd, parts, hparts, apack, wsend)


def combine_kernel(hot_ref, rbuf, rhot, gate_ref, ids_ref, slots_ref, wrecv, apool, out_ref, back_ref, hup_ref, hdn_ref):
    hot = hot_ref[0]
    r = iota((128, 1024), 1)
    code = ((r // 16) % 32) * CAP + (r // 4) % 2
    is_back = (r // 8) % 2
    quarter = r % 4
    hr = iota((128, 64), 1)
    hcode = (hr // 4) % 4
    h_is_back = (hr // 16) % 2
    hquarter = hr % 4
    sel, hsel = [], []
    for c in range(2):
        ids = ids_ref[:, c : c + 1]
        slot = slots_ref[:, c : c + 1]
        is_hot = ids == hot
        place = jnp.where(jnp.logical_and(jnp.logical_not(is_hot), slot < CAP), ids * CAP + slot, -1)
        hplace = jnp.where(jnp.logical_and(is_hot, slot < HCAP), slot, -1)
        sel.append(code == place)
        hsel.append(hcode == hplace)
    data = rbuf[...]
    hdata = rhot[...]

    def pick(s, hs, q, kind):
        m = ones_where(jnp.logical_and(jnp.logical_and(s, quarter == q), is_back == kind))
        hm = ones_where(jnp.logical_and(jnp.logical_and(hs, hquarter == q), h_is_back == kind))
        return dot(m, data) + dot(hm, hdata)

    either = jnp.logical_or(sel[0], sel[1])
    heither = jnp.logical_or(hsel[0], hsel[1])
    for q in range(4):
        cols = slice(q * 512, (q + 1) * 512)
        out = gate_ref[:, 0:1] * pick(sel[0], hsel[0], q, 0) + gate_ref[:, 1:2] * pick(sel[1], hsel[1], q, 0)
        out_ref[:, cols] = out.astype(BF)
        back_ref[:, cols] = pick(either, heither, q, 1).astype(BF)
    w = wrecv[...]
    hup_ref[...] = dot_tn(w, apool[:, 0:512])[0:64]
    hdn_ref[...] = dot_tn(w, apool[:, 512:1024])[64:128]


def combine(hot_index, rbuf, rhot, gate, ids, slots, wrecv, apool):
    return pl.pallas_call(
        combine_kernel,
        out_shape=(sds((128, 2048)), sds((128, 2048)), sds((64, 512), F32), sds((64, 512), F32)),
        in_specs=[SM] + [VM] * 7,
        out_specs=(VM,) * 4,
        compiler_params=pltpu.CompilerParams(vmem_limit_bytes=LIMIT),
        name="combine",
    )(hot_index, rbuf, rhot, gate, ids, slots, wrecv, apool)


def on_device(tokens, cotangent, gate_probs, expert_ids, route_slots, hot_mask, w_up, w_down):
    up, down = w_up[0], w_down[0]
    codes = jnp.arange(hot_mask.shape[0], dtype=jnp.int32)
    hot_index = jnp.sum(hot_mask * codes).reshape(1)
    me = lax.axis_index("expert")
    partner = me + 1 - 2 * (me % 2)
    flags = jnp.stack([hot_index[0] == me, hot_index[0] == partner]).astype(F32)
    disp, hrow = pack(hot_index, tokens, cotangent, gate_probs, expert_ids.T, route_slots.T)
    buf, hbuf, uph, dnh = first_exchange(flags, disp.reshape(32, 16, 512), hrow, up, down)
    gu, gd, parts, hparts, apack, wsend = experts(
        buf.reshape(4096, 512), up, down, hbuf.reshape(256, 512), uph, dnh
    )
    ogu, ogd, rbuf, rhot, apool, wrecv = second_exchange(
        gu, gd, parts.reshape(4, 64, 16, 512), hparts.reshape(4, 2, 32, 512), apack, wsend
    )
    layer_out, grad_tokens, hup, hdn = combine(
        hot_index, rbuf.reshape(1024, 512), rhot.reshape(64, 512), gate_probs, expert_ids, route_slots,
        wrecv.reshape(1024, 128), apool.reshape(1024, 1024),
    )
    is_hot = (hot_mask > 0)[:, None, None]
    grad_up = jnp.where(is_hot, hup.astype(BF)[None], ogu)
    grad_down = jnp.where(is_hot, hdn.astype(BF)[None], ogd)
    return (layer_out, grad_tokens, grad_up, grad_down)


def solution(mesh):
    placed = (
        P(("dp", "expert"), None),
        P(("dp", "expert"), None),
        P(("dp", "expert"), None),
        P(("dp", "expert"), None),
        P(("dp", "expert"), None),
        P(),
        P("expert", None, "dp"),
        P("expert", "dp", None),
    )
    return jax.shard_map(
        on_device,
        mesh=mesh,
        in_specs=placed,
        out_specs=(
            P(("dp", "expert"), None),
            P(("dp", "expert"), None),
            P(None, "expert", "dp"),
            P(None, "expert", "dp"),
        ),
        check_vma=False,
    )
```

time: 650 us -> 312 us (0.48)
  the two profiles are of different devices: /device:TPU:1 before, /device:TPU:163 now
where the time goes in v1:
time: 312 us; the launch traced here: 311 us
  Pallas kernels  276 us (88%)
  local copies, waits for them, and re-layouts  26.2 us (8%)
  other arithmetic  7.24 us (2%)
    pallas_call x1, Pallas kernels, second_exchange(): pl.pallas_call(second_kernel, out_shape=(sds((32, 64, 512)), sds((32, 64,...  159 us
    pallas_call x1, Pallas kernels, first_exchange(): pl.pallas_call(first_kernel, out_shape=(sds((4, 64, 16, 512)), sds((4, 2,...  81.2 us
    unnamed x47, local copies, waits for them, and re-layouts  26.2 us
    pallas_call x1, Pallas kernels, experts(): pl.pallas_call(expert_kernel, out_shape=(sds((2048, 512)), sds((2048, 512...  25.3 us

profile of v1, /device:TPU:163, one launch (start us, length us, event | category | flops | bytes accessed | tf_op | source)
XLA Modules:
  0.0 311.2 jit_solution(13745421662522285494)
XLA Ops:
  0.6 1.3 multiply_reduce_fusion
  3.2 0.1 add_convert_fusion.flags
  3.3 1.4 copy.12.gate_ref
  4.7 4.8 %pack_rows.1 = (bf16[512,512]{1,0:T(8,128)(2,1)}, bf16[32,512]{1,0:T(8,128)(2,1)}) custom-call(s32[1]{0:T(128)} %bitcast.hot_ref, bf16[128,2048]{1,0:T(8,128)(2,1)} %tokens_ref.1, bf16[128,2048]{1,0:T(8,128)(2,1)} %cot_ref.1, f32[128,2]{1,0:T(8,128)} %copy.12.gate_ref, s32[2,128]{1,0:T(2,128)} %bitcast.29, s32[2,128]{1,0:T(2,128)} %bitcast.30), custom_call_target="tpu_custom_call" | custom-call | tf_op jit(solution)/shard_map/pack_rows/pallas_call | solution.py:92
  9.5 1.6 copy-done
  11.1 0.0 copy-start.1
  11.1 1.6 copy-done.1
  12.7 0.0 copy-start.11
  12.7 1.0 copy-done.11
  13.7 0.0 copy-start.18
  13.7 0.8 copy-done.18
  14.5 81.2 %first_exchange.1 = (bf16[4,64,16,512]{3,2,1,0:T(8,128)(2,1)S(1)}, bf16[4,2,32,512]{3,2,1,0:T(8,128)(2,1)S(1)}, bf16[2048,512]{1,0:T(8,128)(2,1)S(1)}, bf16[512,2048]{1,0:T(8,128)(2,1)S(1)}) custom-call(f32[2]{0:T(128)S(1)} %add_convert_fusion.flags, bf16[32,16,512]{2,1,0:T(8,128)(2,1)S(1)} %bitcast.24, bf16[32,512]{1,0:T(8,128)(2,1)S(1)} %copy-done.18, ...), custom_call_target="tpu_custom_call" | custom-call | tf_op jit(solution)/shard_map/first_exchange/pallas_call | solution.py:345
  95.6 0.0 copy-start.2
  95.6 1.9 copy-done.2
  97.6 0.0 copy-start.6
  97.6 1.3 copy-done.6
  98.9 0.0 copy-start.7
  98.9 1.3 copy-done.7
  100.2 0.7 copy-done.14
  100.9 25.3 %experts.1 = (bf16[2048,512]{1,0:T(8,128)(2,1)}, bf16[2048,512]{1,0:T(8,128)(2,1)}, bf16[4096,512]{1,0:T(8,128)(2,1)}, bf16[256,512]{1,0:T(8,128)(2,1)}, bf16[32...) custom-call(bf16[4096,512]{1,0:T(8,128)(2,1)} %bitcast.20, bf16[2048,512]{1,0:T(8,128)(2,1)} %bitcast.16, ...), custom_call_target="tpu_custom_call" | custom-call | tf_op jit(solution)/shard_map/experts/pallas_call | solution.py:459
  126.2 2.2 copy-done.3
  128.4 0.0 copy-start.4
  128.4 1.6 copy-done.4
  130.0 1.6 copy-done.5
  131.6 0.0 copy-start.12
  131.6 0.9 copy-done.12
  132.5 0.0 copy-start.13
  132.6 0.9 copy-done.13
  133.5 0.0 copy-start.17
  133.5 0.8 copy-done.17
  134.3 0.0 copy-start.19
  134.3 0.0 copy-start.20
  134.3 158.6 %second_exchange.1 = (bf16[32,64,512]{2,1,0:T(8,128)(2,1)S(1)}, bf16[32,64,512]{2,1,0:T(8,128)(2,1)S(1)}, bf16[64,16,512]{2,1,0:T(8,128)(2,1)S(1)}, bf16[2,32,51...) custom-call(bf16[2048,512]{1,0:T(8,128)(2,1)S(1)} %copy-done.4, ...), custom_call_target="tpu_custom_call" | custom-call | tf_op jit(solution)/shard_map/second_exchange/pallas_call | solution.py:593
  292.9 0.0 copy-start.8
  292.9 1.3 copy-done.8
  294.3 1.3 copy-done.9
  295.6 1.0 copy-done.10
  296.6 0.7 copy-done.15
  297.3 0.6 copy-done.16
  297.9 0.0 copy-done.19
  297.9 0.7 copy.14.ids_ref
  298.6 0.0 copy-done.20
  298.6 0.7 copy.15.slots_ref
  299.4 6.0 %combine.1 = (bf16[128,2048]{1,0:T(8,128)(2,1)}, bf16[128,2048]{1,0:T(8,128)(2,1)}, f32[64,512]{1,0:T(8,128)}, f32[64,512]{1,0:T(8,128)}) custom-call(s32[1]{0:T(128)} %bitcast.hot_ref, bf16[1024,512]{1,0:T(8,128)(2,1)} %bitcast.23, bf16[64,512]{1,0:T(8,128)(2,1)} %bitcast.28, f32[128,2]{1,0:T(8,128)} %copy.12.gate_ref, s32[128,2]{1,0:T(8,128)} %copy.14.ids_ref, ...), custom_call_target="tpu_custom_call" | custom-call | tf_op jit(solution)/shard_map/combine/pallas_call | solution.py:657
  305.3 0.9 convert_element_type.10
  306.3 0.9 convert_element_type.11
  307.2 0.0 copy-done.21
  307.2 4.0 %broadcast_select_fusion = (bf16[32,64,512]{2,1,0:T(8,128)(2,1)}, bf16[32,64,512]{2,1,0:T(8,128)(2,1)}) fusion(bf16[32,64,512]{2,1,0:T(8,128)(2,1)} %copy-done.9, pred[32]{0:T(512)(128)(4,1)S(1)} %broadcast_compare_fusion, bf16[64,512]{1,0:T(8,128)(2,1)S(1)} %convert_element_type.11, bf16[32,64,512]{2,1,0:T(8,128)(2,1)S(1)} %get-tuple-element.45, ...), kind=kLoop, calls=%fused_computation | loop fusion | flops 2097152 | bytes 8519712 | tf_op jit(solution)/shard_map/jit(_where)/select_n | solution.py:688
  (10 shorter events, 0.0 us)
Async XLA Ops:
  9.5 1.6 copy-start
  11.1 1.6 copy-start.1
  12.7 1.0 copy-start.11
  13.7 0.8 copy-start.18
  95.6 1.9 copy-start.2
  97.6 1.3 copy-start.6
  98.9 1.3 copy-start.7
  100.2 0.7 copy-start.14
  126.2 2.2 copy-start.3
  128.4 1.6 copy-start.4
  130.0 1.6 copy-start.5
  131.6 0.9 copy-start.12
  132.5 0.9 copy-start.13
  133.5 0.8 copy-start.17
  134.3 163.6 %copy-start.19 = (s32[128,2]{0,1:T(2,128)S(1)}, s32[128,2]{0,1:T(2,128)}, u32[]{:S(2)}) copy-start(s32[128,2]{0,1:T(2,128)} %param.11) | copy-start | bytes 3076
  134.3 164.3 %copy-start.20 = (s32[128,2]{0,1:T(2,128)S(1)}, s32[128,2]{0,1:T(2,128)}, u32[]{:S(2)}) copy-start(s32[128,2]{0,1:T(2,128)} %param.12) | copy-start | bytes 3076
  292.9 1.3 copy-start.8
  294.3 1.3 copy-start.9
  295.6 1.0 copy-start.10
  296.6 0.7 copy-start.15
  297.3 0.6 copy-start.16
  297.9 9.3 %copy-start.21 = (s32[32]{0:T(128)S(1)}, s32[32]{0:T(128)}, u32[]{:S(2)}) copy-start(s32[32]{0:T(128)} %param.13) | copy-start | bytes 388

commit v2 on v0

v2 whole, which is shorter than its diff:
```python
import functools

import jax
import jax.numpy as jnp
from jax import lax
from jax.experimental import pallas as pl
from jax.experimental.pallas import tpu as pltpu
from jax.sharding import PartitionSpec as P

CAP = 2
HCAP = 4
MESH = pl.DeviceIdType.MESH
BF = jnp.bfloat16
F32 = jnp.float32
ANY = pl.BlockSpec(memory_space=pl.ANY)
VM = pl.BlockSpec(memory_space=pltpu.VMEM)
SM = pl.BlockSpec(memory_space=pltpu.SMEM)
DMA = pltpu.SemaphoreType.DMA
Z_OFFSETS = (0, 1, 7, 2, 6, 3, 5, 4)
LIMIT = 60 * 1024 * 1024


def sds(shape, dtype=BF):
    return jax.ShapeDtypeStruct(shape, dtype)


def iota(shape, dim):
    return lax.broadcasted_iota(jnp.int32, shape, dim)


def dot(a, b):
    return jnp.dot(a, b, preferred_element_type=F32)


def dot_nt(a, b):
    return lax.dot_general(a, b, (((1,), (1,)), ((), ())), preferred_element_type=F32)


def dot_tn(a, b):
    return lax.dot_general(a, b, (((0,), (0,)), ((), ())), preferred_element_type=F32)


def ones_where(cond):
    return jnp.where(cond, 1.0, 0.0).astype(BF)


class Place:
    def __init__(self):
        self.dp = lax.axis_index("dp")
        self.e = lax.axis_index("expert")
        self.h = self.dp // 4
        self.y = self.dp % 4
        self.z = self.e // 8
        self.x = (self.e // 2) % 4
        self.c = self.e % 2
        self.me = self.h * 32 + self.e
        self.group = self.me // 8

    def at_y(self, y):
        return (self.h * 4 + y, self.e)

    def at_x(self, x):
        return (self.dp, self.z * 8 + x * 2 + self.c)

    def at_z(self, z):
        return (self.dp, z * 8 + self.x * 2 + self.c)

    def partner(self):
        return (self.dp, self.e + 1 - 2 * self.c)

    def at_peer(self, p):
        return ((p // 32) * 4 + self.y, p % 32)


def send(src, dst, ssem, rsem, to):
    copy = pltpu.make_async_remote_copy(
        src_ref=src, dst_ref=dst, send_sem=ssem, recv_sem=rsem, device_id=to, device_id_type=MESH
    )
    copy.start()


def local(src, dst, sem):
    pltpu.make_async_copy(src, dst, sem).start()


def wait(ref, sem):
    pltpu.make_async_copy(ref, ref, sem).wait()


def rows(start, size):
    return pl.ds(pl.multiple_of(start, 16), size)


def gelu_pair(preact):
    normal_cdf = 0.5 * (1.0 + lax.erf(preact * 0.7071067811865476))
    density = jnp.exp(-0.5 * preact * preact) * 0.3989422804014327
    return (preact * normal_cdf, normal_cdf + preact * density)


def order_matrix(src_count, slot_count):
    r = iota((256, 256), 0)
    k = iota((256, 256), 1)
    slot = r % slot_count
    src = (r // slot_count) % src_count
    q = (r // 32) % 4
    a = r // 128
    return ones_where(k == src * (8 * slot_count) + a * (4 * slot_count) + slot * 4 + q)


def to_column(row):
    wide = row.shape[1]
    same = iota((wide, wide), 0) == iota((wide, wide), 1)
    return jnp.sum(jnp.where(same, row, jnp.zeros_like(row)), axis=1, keepdims=True)


def places_of(ids, slot, hot):
    is_hot = ids == hot
    normal = jnp.where(jnp.logical_and(jnp.logical_not(is_hot), slot < CAP), ids * CAP + slot, -1)
    special = jnp.where(jnp.logical_and(is_hot, slot < HCAP), slot, -1)
    return normal, special


def pack_rows(hot, tokens, cot, gate_cols, ids, slots, disp, hrow):
    r = iota((512, 128), 0)
    code = (r // 16) * CAP + (r // 4) % 2
    is_grad = (r // 8) % 2
    quarter = r % 4
    hr = iota((32, 128), 0)
    hcode = (hr // 4) % 4
    h_is_grad = hr // 16
    hquarter = hr % 4
    sel, hsel = [], []
    for k in range(2):
        normal, special = places_of(ids[k : k + 1, :], slots[k : k + 1, :], hot)
        sel.append(code == normal)
        hsel.append(hcode == special)
    either = jnp.logical_or(sel[0], sel[1])
    heither = jnp.logical_or(hsel[0], hsel[1])
    out = jnp.zeros((512, 512), F32)
    hout = jnp.zeros((32, 512), F32)
    for q in range(4):
        cols = slice(q * 512, (q + 1) * 512)
        wide = cot[:, cols].astype(F32)
        parts = (
            (tokens[:, cols], either, heither, 0),
            ((gate_cols[0] * wide).astype(BF), sel[0], hsel[0], 1),
            ((gate_cols[1] * wide).astype(BF), sel[1], hsel[1], 1),
        )
        for data, s, hs, kind in parts:
            m = ones_where(jnp.logical_and(jnp.logical_and(s, quarter == q), is_grad == kind))
            out += dot(m, data)
            hm = ones_where(jnp.logical_and(jnp.logical_and(hs, hquarter == q), h_is_grad == kind))
            hout += dot(hm, data)
    disp[...] = out.astype(BF).reshape(32, 16, 512)
    hrow[...] = hout.astype(BF)


def combine_rows(hot, rbuf, rhot, gate_cols, id_cols, slot_cols, out_ref, back_ref):
    r = iota((128, 1024), 1)
    code = ((r // 16) % 32) * CAP + (r // 4) % 2
    is_back = (r // 8) % 2
    quarter = r % 4
    hr = iota((128, 64), 1)
    hcode = (hr // 4) % 4
    h_is_back = (hr // 16) % 2
    hquarter = hr % 4
    sel, hsel = [], []
    for k in range(2):
        normal, special = places_of(id_cols[k], slot_cols[k], hot)
        sel.append(code == normal)
        hsel.append(hcode == special)
    data = rbuf[...].reshape(1024, 512)
    hdata = rhot[...].reshape(64, 512)

    def pick(s, hs, q, kind):
        m = ones_where(jnp.logical_and(jnp.logical_and(s, quarter == q), is_back == kind))
        hm = ones_where(jnp.logical_and(jnp.logical_and(hs, hquarter == q), h_is_back == kind))
        return dot(m, data) + dot(hm, hdata)

    either = jnp.logical_or(sel[0], sel[1])
    heither = jnp.logical_or(hsel[0], hsel[1])
    for q in range(4):
        cols = slice(q * 512, (q + 1) * 512)
        out = gate_cols[0] * pick(sel[0], hsel[0], q, 0) + gate_cols[1] * pick(sel[1], hsel[1], q, 0)
        out_ref[:, cols] = out.astype(BF)
        back_ref[:, cols] = pick(either, heither, q, 1).astype(BF)


def layer_kernel(
    mask_ref, tokens, cot, gate_ref, ids_ref, slots_ref, up, down,
    out_ref, back_ref, hup_ref, hdn_ref, ogu, ogd,
    disp, hrow, buf, hbuf, upv, dnv, uph, dnh,
    p_up, p_dn, o_up, o_dn, m_up, m_dn, r_up, r_dn, t_up, t_dn,
    xs, act_s, pre_s, ys, gu, gd, parts, hparts, apack, wsend,
    m, r, ret, rbuf, hr, hret, rhot, apool, wrecv,
    load_s, disp_s, disp_r, y_s, y_r, y_f, h_s, h_r, hy_s, hy_r,
    s1_s, s1_r, s1_l, s2_s, s2_m, s2_raw, s2_acc, s3_s, s3_r, s4_s, s4_r, s4_l, s5_s, s5_r, s5_f, s6_s, s6_r,
    g_s, g_r, w_s, w_r, m_s, m_r, raw_s, raw_r, acc_s, acc_r, ret_s, ret_r,
    hp_s, hp_r, hret_s, hret_r, az_s, az_r, ax_s, ax_r, ac_s, ac_r,
):
    at = Place()
    y, x, z, c = at.y, at.x, at.z, at.c
    yr, yl, yo = (y + 1) % 4, (y + 3) % 4, (y + 2) % 4
    xr, xl, xo = (x + 1) % 4, (x + 3) % 4, (x + 2) % 4

    barrier = pltpu.get_barrier_semaphore()

    def greet(k, _):
        pl.semaphore_signal(barrier, inc=1, device_id=at.at_peer((at.me + k) % 64), device_id_type=MESH)
        return 0

    lax.fori_loop(1, 64, greet, 0)
    for k in range(1, 4):
        pl.semaphore_signal(barrier, inc=1, device_id=at.at_y((y + k) % 4), device_id_type=MESH)

    arrays = ((up, o_up, p_up, 1024), (down, o_dn, p_dn, 256))
    for i, (w, own, _, n) in enumerate(arrays):
        local(w.at[rows(c * n, n)], own, s1_l.at[i])
    local(up, upv, load_s.at[0])
    local(down, dnv, load_s.at[1])

    hot = mask_ref[0] * 0
    for k in range(1, 32):
        hot += mask_ref[k] * k
    f_own = jnp.where(hot == at.e, 1.0, 0.0)
    f_other = jnp.where(hot == at.e + 1 - 2 * c, 1.0, 0.0)
    gate_cols = [to_column(gate_ref[k : k + 1, :]) for k in range(2)]
    pack_rows(hot, tokens, cot, gate_cols, ids_ref, slots_ref, disp, hrow)

    pl.semaphore_wait(barrier, 66)

    for i, (w, _, other, n) in enumerate(arrays):
        send(w.at[rows((1 - c) * n, n)], other, s1_s.at[i], s1_r.at[i], at.partner())

    local(disp.at[at.e], buf.at[y, at.me], disp_r.at[at.group])
    groups = [(at.group + off) % 8 for off in Z_OFFSETS]
    for i, off in enumerate(Z_OFFSETS):

        def dispatch(k, _, g=groups[i]):
            p = g * 8 + (at.me + k) % 8
            send(disp.at[p % 32], buf.at[y, at.me], disp_s, disp_r.at[at.group], at.at_peer(p))
            return 0

        lax.fori_loop(1 if i == 0 else 0, 8, dispatch, 0)
    local(hrow, hbuf.at[y, at.h], h_r.at[0])
    send(hrow, hbuf.at[y, at.h], h_s, h_r.at[1], at.at_peer((at.me + 32) % 64))

    for i, (w, own, other, n) in enumerate(arrays):
        wait(own, s1_l.at[i])
        wait(other, s1_r.at[i])
    for own, other, n in ((o_up, p_up, 1024), (o_dn, p_dn, 256)):

        def choose(k, _, own=own, other=other, n=n):
            s = rows(k * (n // 16), n // 16)
            own[s] = (own[s].astype(F32) * f_own + other[s].astype(F32) * f_other).astype(BF)
            return 0

        lax.fori_loop(0, 16, choose, 0)

    ring = ((o_up, m_up, r_up, t_up, 128), (o_dn, m_dn, r_dn, t_dn, 32))
    for i, (o, mm, rr, t, n) in enumerate(ring):
        send(o.at[rows(xo * 2 * n, n)], mm.at[0], s2_s.at[i, 0], s2_m.at[i, 0], at.at_x(xr))
        send(o.at[rows(xo * 2 * n + n, n)], mm.at[1], s2_s.at[i, 1], s2_m.at[i, 1], at.at_x(xl))
        send(o.at[rows(xr * 2 * n + n, n)], rr.at[0, pl.ds(n, n)], s2_s.at[i, 2], s2_raw.at[i, 0], at.at_x(xr))
        send(o.at[rows(xl * 2 * n, n)], rr.at[1, pl.ds(0, n)], s2_s.at[i, 3], s2_raw.at[i, 1], at.at_x(xl))

    def slab(of_y, g):
        return buf.at[of_y, pl.ds(g * 8, 8)]

    def pass_on(i):
        g = groups[i]
        wait(slab(y, g), disp_r.at[g])
        send(slab(y, g), slab(y, g), y_s, y_r.at[0, i], at.at_y(yr))
        send(slab(y, g), slab(y, g), y_s, y_r.at[1, i], at.at_y(yl))

    def forward(i):
        g = groups[i]
        wait(slab(yl, g), y_r.at[0, i])
        if i % 2 == 0:
            send(slab(yl, g), slab(yl, g), y_s, y_f.at[i], at.at_y(yr))
        wait(slab(yr, g), y_r.at[1, i])
        if i % 2 == 1:
            send(slab(yr, g), slab(yr, g), y_s, y_f.at[i], at.at_y(yl))

    order = order_matrix(16, 2)

    def hidden(s):
        def sort_rows(b, _):
            data = buf[s, pl.ds(b * 16, 16)].reshape(256, 512)
            block = dot(order, data).astype(BF)
            for k in range(8):
                xs[k, rows(s * 128 + b * 32, 32)] = block[k * 32 : (k + 1) * 32]
            return 0

        lax.fori_loop(0, 4, sort_rows, 0)
        at_s = rows(s * 128, 128)
        preact = dot(xs[0, at_s], upv[0:512])
        dact = dot_nt(xs[4, at_s], dnv[:, 0:512])
        for q in range(1, 4):
            preact += dot(xs[q, at_s], upv[q * 512 : (q + 1) * 512])
            dact += dot_nt(xs[4 + q, at_s], dnv[:, q * 512 : (q + 1) * 512])
        value, slope = gelu_pair(preact)
        act_s[at_s] = value.astype(BF)
        pre_s[at_s] = (dact * slope).astype(BF)

    for i in range(5):
        pass_on(i)

    for i, (o, mm, rr, t, n) in enumerate(ring):
        wait(mm.at[0], s2_m.at[i, 0])
        mm[0] = mm[0] + o[rows(xr * 2 * n, n)]
        send(mm.at[0], rr.at[0, pl.ds(0, n)], s2_s.at[i, 4], s2_acc.at[i, 0], at.at_x(xr))
        wait(mm.at[1], s2_m.at[i, 1])
        mm[1] = mm[1] + o[rows(xl * 2 * n + n, n)]
        send(mm.at[1], rr.at[1, pl.ds(n, n)], s2_s.at[i, 5], s2_acc.at[i, 1], at.at_x(xl))

    for i in range(5, 8):
        pass_on(i)

    wait(hbuf.at[y, at.h], h_r.at[0])
    wait(hbuf.at[y, 1 - at.h], h_r.at[1])
    for k in range(1, 4):
        send(hbuf.at[y], hbuf.at[y], hy_s, hy_r, at.at_y((y + k) % 4))

    for i in range(2):
        forward(i)
    wait(upv, load_s.at[0])
    wait(dnv, load_s.at[1])
    hidden(y)
    for i in range(2, 4):
        forward(i)

    for i, (o, mm, rr, t, n) in enumerate(ring):
        for side, raw, acc in ((0, pl.ds(n, n), pl.ds(0, n)), (1, pl.ds(0, n), pl.ds(n, n))):
            wait(rr.at[side, raw], s2_raw.at[i, side])
            wait(rr.at[side, acc], s2_acc.at[i, side])
        rr[0] = rr[0] + rr[1] + o[rows(x * 2 * n, 2 * n)]
        w = n // 2
        for k in range(1, 4):
            zz = (z + k) % 4
            send(rr.at[0, rows(zz * w, w)], t.at[k - 1], s3_s.at[i, k - 1], s3_r.at[i, k - 1], at.at_z(zz))

    for i in range(4, 8):
        forward(i)

    full = ((uph, t_up, r_up, 64), (dnh, t_dn, r_dn, 16))
    for i, (dst, t, rr, w) in enumerate(full):
        for k in range(3):
            wait(t.at[k], s3_r.at[i, k])
        t[3] = t[0] + t[1] + t[2] + rr[0, rows(z * w, w)]
        place = rows(c * 16 * w + x * 4 * w + z * w, w)
        local(t.at[3], dst.at[place], s4_l.at[i])
        for k in range(1, 4):
            send(t.at[3], dst.at[place], s4_s.at[i, k - 1], s4_r.at[i, k - 1], at.at_z((z + k) % 4))

    hidden(yl)
    hidden(yr)

    wait(hbuf.at[pl.ds(0, 3)], hy_r)
    horder = order_matrix(8, 4)
    hx = dot(horder, hbuf[...].reshape(256, 512)).astype(BF)
    hx = [hx[k * 32 : (k + 1) * 32] for k in range(8)]
    i0 = iota((128, 128), 0)
    j0 = iota((128, 128), 1)
    for odd in range(2):
        take_in = ones_where(jnp.logical_and(j0 < 64, i0 == j0 + 64 * odd))
        take_grad = ones_where(jnp.logical_and(j0 >= 64, i0 == j0 - 64 + 64 * odd))
        for b in range(16):
            q, o = b // 4, (b % 4) * 128
            block = dot(hx[q][:, o : o + 128], take_in) + dot(hx[4 + q][:, o : o + 128], take_grad)
            wsend[2 * b + odd] = block.astype(BF)
    local(wsend.at[at.e], wrecv.at[at.e], w_r)

    def widths(k, _):
        e = (at.e + k) % 32
        send(wsend.at[e], wrecv.at[at.e], w_s, w_r, (at.dp, e))
        return 0

    lax.fori_loop(1, 32, widths, 0)

    def half_of(dst, w):
        return lambda xx, b: dst.at[rows(c * 16 * w + xx * 4 * w + b * 2 * w, 2 * w)]

    def quarter_of(dst, w, xx):
        return dst.at[rows(c * 16 * w + xx * 4 * w, 4 * w)]

    for i, (dst, t, rr, w) in enumerate(full):
        wait(t.at[3], s4_l.at[i])
        for k in range(3):
            wait(t.at[3], s4_r.at[i, k])
        half = half_of(dst, w)
        for b in range(2):
            send(half(x, b), half(x, b), s5_s.at[i, b], s5_r.at[i, 0, b], at.at_x(xr))
            send(half(x, b), half(x, b), s5_s.at[i, 2 + b], s5_r.at[i, 1, b], at.at_x(xl))
        send(quarter_of(dst, w, x), quarter_of(dst, w, x), s6_s.at[i, 0], s6_r.at[i, 0], at.partner())

    for i in range(8):
        wait(slab(yo, groups[i]), y_f.at[i])
    hidden(yo)

    local_at = rows(at.e * 64, 64)

    def gradients(q):
        here = rows(q * 512, 512)
        gu[here] = dot_tn(xs[q], pre_s[...]).astype(BF)
        gd[here] = dot_tn(xs[4 + q], act_s[...]).astype(BF)

    def give_gradients(k, _, q):
        e = q * 8 + (at.e + k) % 8
        to = (at.dp, e)
        send(gu.at[rows(e * 64, 64)], ogu.at[at.e], g_s.at[0], g_r.at[0], to)
        send(gd.at[rows(e * 64, 64)], ogd.at[at.e], g_s.at[1], g_r.at[1], to)
        return 0

    def partial(s):
        at_s = rows(s * 128, 128)
        for q in range(4):
            cols = slice(q * 512, (q + 1) * 512)
            ys[q] = dot(act_s[at_s], dnv[:, cols]).astype(BF)
            ys[4 + q] = dot_nt(pre_s[at_s], upv[cols, :]).astype(BF)

        def unsort_rows(b, _):
            block = jnp.concatenate([ys[k, rows(b * 32, 32)] for k in range(8)], axis=0)
            parts[s, pl.ds(b * 16, 16)] = dot_tn(order, block).astype(BF).reshape(16, 16, 512)
            return 0

        lax.fori_loop(0, 4, unsort_rows, 0)

    def part(of_y, g):
        return parts.at[of_y, pl.ds(g * 8, 8)]

    for k in (2, 1):
        q = (z + k) % 4
        gradients(q)
        lax.fori_loop(0, 8, functools.partial(give_gradients, q=q), 0)
    partial(yo)
    for i in range(4):
        send(part(yo, i), m.at[0, i], m_s, m_r.at[0, i], at.at_y(yr))
        send(part(yo, 4 + i), m.at[1, i], m_s, m_r.at[1, i], at.at_y(yl))
    q = (z + 3) % 4
    gradients(q)
    lax.fori_loop(0, 8, functools.partial(give_gradients, q=q), 0)
    for s, to, first, side in ((yr, yr, 4, 0), (yl, yl, 0, 1)):
        partial(s)
        for i in range(4):
            send(part(s, first + i), r.at[side, first + i], raw_s, raw_r.at[side, i], at.at_y(to))
    gradients(z)
    local(gu.at[local_at], ogu.at[at.e], g_r.at[0])
    local(gd.at[local_at], ogd.at[at.e], g_r.at[1])
    lax.fori_loop(1, 8, functools.partial(give_gradients, q=z), 0)

    for i, (dst, t, rr, w) in enumerate(full):
        half = half_of(dst, w)
        wait(half(xl, 0), s5_r.at[i, 0, 0])
        send(half(xl, 0), half(xl, 0), s5_s.at[i, 4], s5_f.at[i, 0], at.at_x(xr))
        wait(half(xr, 1), s5_r.at[i, 1, 1])
        send(half(xr, 1), half(xr, 1), s5_s.at[i, 5], s5_f.at[i, 1], at.at_x(xl))

    for i in range(4):
        wait(m.at[0, i], m_r.at[0, i])
        m[0, i] = (m[0, i].astype(F32) + parts[yr, pl.ds(i * 8, 8)].astype(F32)).astype(BF)
        send(m.at[0, i], r.at[0, i], acc_s, acc_r.at[0, i], at.at_y(yr))
        wait(m.at[1, i], m_r.at[1, i])
        m[1, i] = (m[1, i].astype(F32) + parts[yl, pl.ds(32 + i * 8, 8)].astype(F32)).astype(BF)
        send(m.at[1, i], r.at[1, 4 + i], acc_s, acc_r.at[1, i], at.at_y(yl))
    partial(y)

    for i, (dst, t, rr, w) in enumerate(full):
        half = half_of(dst, w)
        wait(half(xl, 1), s5_r.at[i, 0, 1])
        wait(half(xr, 0), s5_r.at[i, 1, 0])
        for k, xx in ((1, xl), (2, xr)):
            send(quarter_of(dst, w, xx), quarter_of(dst, w, xx), s6_s.at[i, k], s6_r.at[i, k], at.partner())
    for i, (dst, t, rr, w) in enumerate(full):
        half = half_of(dst, w)
        wait(half(xo, 0), s5_f.at[i, 0])
        wait(half(xo, 1), s5_f.at[i, 1])
        send(quarter_of(dst, w, xo), quarter_of(dst, w, xo), s6_s.at[i, 3], s6_r.at[i, 3], at.partner())
    for i, (dst, t, rr, w) in enumerate(full):
        for k in range(4):
            wait(dst.at[pl.ds(0, 4 * w)], s6_r.at[i, k])

    preact = dot(hx[0], uph[0:512])
    dact = dot_nt(hx[4], dnh[:, 0:512])
    for q in range(1, 4):
        preact += dot(hx[q], uph[q * 512 : (q + 1) * 512])
        dact += dot_nt(hx[4 + q], dnh[:, q * 512 : (q + 1) * 512])
    value, slope = gelu_pair(preact)
    hact = value.astype(BF)
    hpre = (dact * slope).astype(BF)
    apack[:, 0:512] = hpre
    apack[:, 512:1024] = hact
    local(apack, apool.at[z, x, c], az_r.at[3])
    for k in range(1, 4):
        send(apack, apool.at[z, x, c], az_s, az_r.at[k - 1], at.at_z((z + k) % 4))
    outs = [dot(hact, dnh[:, q * 512 : (q + 1) * 512]).astype(BF) for q in range(4)]
    backs = [dot_nt(hpre, uph[q * 512 : (q + 1) * 512, :]).astype(BF) for q in range(4)]
    hout = dot_tn(horder, jnp.concatenate(outs + backs, axis=0)).astype(BF)
    hparts[...] = hout.reshape(4, 2, 32, 512)
    for k in range(1, 4):
        yy = (y + k) % 4
        send(hparts.at[yy], hr.at[k - 1], hp_s, hp_r.at[k - 1], at.at_y(yy))

    for i in range(8):
        side_raw, side_acc = (1, 0) if i < 4 else (0, 1)
        wait(r.at[side_raw, i], raw_r.at[side_raw, i % 4])
        wait(r.at[side_acc, i], acc_r.at[side_acc, i % 4])
        ret[pl.ds(i * 8, 8)] = (
            parts[y, pl.ds(i * 8, 8)].astype(F32) + r[0, i].astype(F32) + r[1, i].astype(F32)
        ).astype(BF)

        def give_back(j, _, i=i):
            p = i * 8 + j

            @pl.when(p != at.me)
            def _():
                send(ret.at[p], rbuf.at[at.me], ret_s, ret_r, at.at_peer(p))

            @pl.when(p == at.me)
            def _():
                local(ret.at[p], rbuf.at[p], ret_r)

            return 0

        lax.fori_loop(0, 8, give_back, 0)

    for k in range(4):
        wait(apack, az_r.at[k])
    for k in range(1, 4):
        send(apool.at[:, x, c], apool.at[:, x, c], ax_s, ax_r.at[k - 1], at.at_x((x + k) % 4))
    for k in range(3):
        wait(hr.at[k], hp_r.at[k])
    hret[...] = (
        hparts[y].astype(F32) + hr[0].astype(F32) + hr[1].astype(F32) + hr[2].astype(F32)
    ).astype(BF)
    local(hret.at[at.h], rhot.at[at.h], hret_r.at[0])
    send(hret.at[1 - at.h], rhot.at[at.h], hret_s, hret_r.at[1], at.at_peer((at.me + 32) % 64))
    for k in range(3):
        wait(apool.at[:, 0, 0], ax_r.at[k])
    send(apool.at[:, :, c], apool.at[:, :, c], ac_s, ac_r, at.partner())

    wait(wrecv, w_r)
    wait(apool.at[:, :, 0], ac_r)
    wide = wrecv[...].reshape(1024, 128)
    pool = apool[...].reshape(1024, 1024)
    hup_ref[...] = dot_tn(wide, pool[:, 0:512])[0:64].astype(BF)
    hdn_ref[...] = dot_tn(wide, pool[:, 512:1024])[64:128].astype(BF)

    wait(rbuf, ret_r)
    wait(rhot.at[0], hret_r.at[0])
    wait(rhot.at[0], hret_r.at[1])
    id_cols = [to_column(ids_ref[k : k + 1, :]) for k in range(2)]
    slot_cols = [to_column(slots_ref[k : k + 1, :]) for k in range(2)]
    combine_rows(hot, rbuf, rhot, gate_cols, id_cols, slot_cols, out_ref, back_ref)

    wait(ogu, g_r.at[0])
    wait(ogd, g_r.at[1])

    for i, (w, own, other, n) in enumerate(arrays):
        wait(own, s1_s.at[i])
    wait(buf.at[0, pl.ds(0, 63)], disp_s)
    wait(buf.at[pl.ds(0, 3)], y_s)
    wait(hbuf.at[pl.ds(0, 3)], hy_s)
    wait(hbuf.at[0, 0], h_s)
    for i, (o, mm, rr, t, n) in enumerate(ring):
        for k in range(6):
            wait(mm.at[0], s2_s.at[i, k])
        for k in range(3):
            wait(t.at[0], s3_s.at[i, k])
            wait(t.at[0], s4_s.at[i, k])
    for i, (dst, t, rr, w) in enumerate(full):
        for k in range(6):
            wait(dst.at[pl.ds(0, 2 * w)], s5_s.at[i, k])
        for k in range(4):
            wait(dst.at[pl.ds(0, 4 * w)], s6_s.at[i, k])
    wait(gu.at[pl.ds(0, 31 * 64)], g_s.at[0])
    wait(gd.at[pl.ds(0, 31 * 64)], g_s.at[1])
    wait(wsend.at[pl.ds(0, 31)], w_s)
    wait(m, m_s)
    wait(m, raw_s)
    wait(m, acc_s)
    wait(ret.at[pl.ds(0, 63)], ret_s)
    wait(hr, hp_s)
    wait(hret.at[0], hret_s)
    wait(apool.at[0, 0:3, 0], az_s)
    wait(apool.at[:, 0:3, 0], ax_s)
    wait(apool.at[:, :, 0], ac_s)


def layer(hot_mask, tokens, cotangent, gate_t, ids_t, slots_t, up, down):
    def vm(*shape):
        return pltpu.VMEM(shape, BF)

    return pl.pallas_call(
        layer_kernel,
        out_shape=(
            sds((128, 2048)), sds((128, 2048)), sds((64, 512)), sds((64, 512)),
            sds((32, 64, 512)), sds((32, 64, 512)),
        ),
        in_specs=[SM, VM, VM, VM, VM, VM, ANY, ANY],
        out_specs=(VM, VM, VM, VM, ANY, ANY),
        scratch_shapes=[
            vm(32, 16, 512), vm(32, 512), vm(4, 64, 16, 512), vm(4, 2, 32, 512),
            vm(2048, 512), vm(512, 2048), vm(2048, 512), vm(512, 2048),
            vm(1024, 512), vm(256, 2048), vm(1024, 512), vm(256, 2048),
            vm(2, 128, 512), vm(2, 32, 2048), vm(2, 256, 512), vm(2, 64, 2048),
            vm(4, 64, 512), vm(4, 16, 2048),
            vm(8, 512, 512), vm(512, 512), vm(512, 512), vm(8, 128, 512),
            vm(2048, 512), vm(2048, 512), vm(4, 64, 16, 512), vm(4, 2, 32, 512),
            vm(32, 1024), vm(32, 32, 128),
            vm(2, 4, 8, 16, 512), vm(2, 8, 8, 16, 512), vm(64, 16, 512), vm(64, 16, 512),
            vm(3, 2, 32, 512), vm(2, 32, 512), vm(2, 32, 512), vm(4, 4, 2, 32, 1024), vm(32, 32, 128),
            DMA((2,)), DMA, DMA((8,)), DMA, DMA((2, 8)), DMA((8,)), DMA, DMA((2,)), DMA, DMA,
            DMA((2,)), DMA((2,)), DMA((2,)),
            DMA((2, 6)), DMA((2, 2)), DMA((2, 2)), DMA((2, 2)),
            DMA((2, 3)), DMA((2, 3)), DMA((2, 3)), DMA((2, 3)), DMA((2,)),
            DMA((2, 6)), DMA((2, 2, 2)), DMA((2, 2)), DMA((2, 4)), DMA((2, 4)),
            DMA((2,)), DMA((2,)), DMA, DMA, DMA, DMA((2, 4)), DMA, DMA((2, 4)), DMA, DMA((2, 4)), DMA, DMA,
            DMA, DMA((3,)), DMA, DMA((2,)), DMA, DMA((4,)), DMA, DMA((3,)), DMA, DMA,
        ],
        compiler_params=pltpu.CompilerParams(
            collective_id=1, has_side_effects=True, vmem_limit_bytes=LIMIT
        ),
        name="layer",
    )(hot_mask, tokens, cotangent, gate_t, ids_t, slots_t, up, down)


def on_device(tokens, cotangent, gate_probs, expert_ids, route_slots, hot_mask, w_up, w_down):
    layer_out, grad_tokens, hup, hdn, ogu, ogd = layer(
        hot_mask, tokens, cotangent, gate_probs.T, expert_ids.T, route_slots.T, w_up[0], w_down[0]
    )
    is_hot = (hot_mask > 0)[:, None, None]
    grad_up = jnp.where(is_hot, hup[None], ogu)
    grad_down = jnp.where(is_hot, hdn[None], ogd)
    return (layer_out, grad_tokens, grad_up, grad_down)


def solution(mesh):
    placed = (
        P(("dp", "expert"), None),
        P(("dp", "expert"), None),
        P(("dp", "expert"), None),
        P(("dp", "expert"), None),
        P(("dp", "expert"), None),
        P(),
        P("expert", None, "dp"),
        P("expert", "dp", None),
    )
    return jax.shard_map(
        on_device,
        mesh=mesh,
        in_specs=placed,
        out_specs=(
            P(("dp", "expert"), None),
            P(("dp", "expert"), None),
            P(None, "expert", "dp"),
            P(None, "expert", "dp"),
        ),
        check_vma=False,
    )
```

time: 650 us -> 215 us (0.33)
  waiting for transfers between devices: 426 us -> 0 us
  Pallas kernels: 0 us -> 205 us
  starting transfers between devices: 64.7 us -> 0 us
  blocking collectives: 52.5 us -> 0 us
  matrix products: 42 us -> 0 us
  local copies, waits for them, and re-layouts: 25.7 us -> 1.59 us
  between operations: 16.8 us -> 0.66 us
  other arithmetic: 16.5 us -> 5.39 us
    pallas_call x0 -> x1, Pallas kernels: none -> 205 us  [layer(): pl.pallas_call(layer_kernel, out_shape=(sds((128, 2048)), sds((128, 2048)...]
    psum x1 -> x0, waiting for transfers between devices: 158 us -> none  [spread(): return lax.psum(jnp.where(mine, shard, jnp.zeros_like(shard)), axis)]
    all_to_all x6 -> x0, waiting for transfers between devices: 141 us -> none  [the longest x1 70.7 us: on_device(): lax.all_to_all(grad_in.astype(jnp.bfloat16).reshape(expert_count, block_r...]
    all_gather x2 -> x0, waiting for transfers between devices: 83.6 us -> none  [side_by_side(): lax.all_gather(both, axis, axis=dim, tiled=True)]
    all_to_all x6 -> x0, starting transfers between devices: 64.3 us -> none  [the longest x1 30.5 us: side_by_side_2(): lax.all_to_all(both, axis, split_axis=split_dim, concat_axis=concat_dim,...]
    unnamed x7 -> x0, waiting for transfers between devices: 43.6 us -> none
    dot_general x20 -> x0, matrix products: 42 us -> none  [the longest x4 12.3 us: contract_rows(): lax.dot_general(left_rows, right_rows, (((0,), (0,)), ((), ())), preferre...]
    all_gather x1 -> x0, blocking collectives: 37.8 us -> none  [side_by_side(): lax.all_gather(both, axis, axis=dim, tiled=True)]
  transfers between devices with their start and end apart: 12 -> 0, of which waited for: 8 -> 0; matrix products, arithmetic and copies ran while one was open for 11% -> 0% of each run, Pallas kernels for 0% -> 0%
where the time goes in v2:
time: 215 us; the launch traced here: 212 us
  Pallas kernels  205 us (95%)
  other arithmetic  5.39 us (3%)
    pallas_call x1, Pallas kernels, layer(): pl.pallas_call(layer_kernel, out_shape=(sds((128, 2048)), sds((128, 2048)...  205 us
    select_n x1, other arithmetic, on_device(): grad_down = jnp.where(is_hot, hdn[None], ogd)  4.73 us

profile of v2, /device:TPU:1, one launch (start us, length us, event | category | flops | bytes accessed | tf_op | source)
XLA Modules:
  0.0 212.3 jit_solution(6835604291932103642)
XLA Ops:
  0.6 0.7 broadcast_compare_fusion
  1.3 204.7 %layer.1 = (bf16[128,2048]{1,0:T(8,128)(2,1)}, bf16[128,2048]{1,0:T(8,128)(2,1)}, bf16[64,512]{1,0:T(8,128)(2,1)}, bf16[64,512]{1,0:T(8,128)(2,1)}, bf16[32,64,5...) custom-call(s32[32]{0:T(128)} %mask_ref.1, bf16[128,2048]{1,0:T(8,128)(2,1)} %tokens.1, bf16[128,2048]{1,0:T(8,128)(2,1)} %cot.1, ...), custom_call_target="tpu_custom_call" | custom-call | tf_op jit(solution)/shard_map/layer/pallas_call | solution.py:594
  206.0 0.0 copy-start.1
  206.0 0.0 copy-start
  206.0 4.7 %broadcast_select_fusion = (bf16[32,64,512]{2,1,0:T(8,128)(2,1)}, bf16[32,64,512]{2,1,0:T(8,128)(2,1)}) fusion(bf16[32,64,512]{2,1,0:T(8,128)(2,1)} %get-tuple-element.15, pred[32]{0:T(512)(128)(4,1)S(1)} %broadcast_compare_fusion, bf16[64,512]{1,0:T(8,128)(2,1)} %get-tuple-element.14, bf16[32,64,512]{2,1,0:T(8,128)(2,1)} %get-tuple-element.13, ...), kind=kLoop, calls=%fused_computation | loop fusion | flops 2097152 | bytes 8519712 | tf_op jit(solution)/shard_map/jit(_where)/select_n | solution.py:634
  210.7 0.0 copy-done.1
  210.7 0.8 copy.14
  211.5 0.0 copy-done
  211.5 0.8 copy.15
Async XLA Ops:
  206.0 4.8 %copy-start.1 = (bf16[128,2048]{1,0:T(8,128)(2,1)S(1)}, bf16[128,2048]{1,0:T(8,128)(2,1)}, u32[]{:S(2)}) copy-start(bf16[128,2048]{1,0:T(8,128)(2,1)} %get-tuple-element.22) | copy-start | bytes 1572868
  206.0 5.5 %copy-start = (bf16[128,2048]{1,0:T(8,128)(2,1)S(1)}, bf16[128,2048]{1,0:T(8,128)(2,1)}, u32[]{:S(2)}) copy-start(bf16[128,2048]{1,0:T(8,128)(2,1)} %get-tuple-element.23) | copy-start | bytes 1572868

commit v3 on v2

--- a/solution.py
+++ b/solution.py
@@ -155,6 +155,30 @@
     hrow[...] = hout.astype(BF)
 
 
+def pack_columns(hot, tokens, cot, gate_cols, ids, slots, edisp):
+    r = iota((512, 128), 0)
+    dest = r // 16
+    z = dest // 8
+    code = ((2 - z // 2) * 8 + dest % 8) * CAP + (r // 4) % 2
+    is_grad = (r // 8) % 2
+    piece = z * 4 + r % 4
+    sel = [code == places_of(ids[k : k + 1, :], slots[k : k + 1, :], hot)[0] for k in range(2)]
+    either = jnp.logical_or(sel[0], sel[1])
+    masks = [
+        jnp.logical_and(s, is_grad == kind) for s, kind in ((either, 0), (sel[0], 1), (sel[1], 1))
+    ]
+    for q in range(4):
+        here = slice(q * 128, (q + 1) * 128)
+        out = jnp.zeros((128, 128), F32)
+        for p in range(4 * q, 4 * q + 4):
+            cols = slice(p * 128, (p + 1) * 128)
+            wide = cot[:, cols].astype(F32)
+            data = (tokens[:, cols], (gate_cols[0] * wide).astype(BF), (gate_cols[1] * wide).astype(BF))
+            for d, mask in zip(data, masks):
+                out += dot(ones_where(jnp.logical_and(mask, piece == p)[here]), d)
+        edisp[q * 8 : (q + 1) * 8] = out.astype(BF).reshape(8, 16, 128)
+
+
 def combine_rows(hot, rbuf, rhot, gate_cols, id_cols, slot_cols, out_ref, back_ref):
     r = iota((128, 1024), 1)
     code = ((r // 16) % 32) * CAP + (r // 4) % 2
@@ -191,12 +215,14 @@
     out_ref, back_ref, hup_ref, hdn_ref, ogu, ogd,
     disp, hrow, buf, hbuf, upv, dnv, uph, dnh,
     p_up, p_dn, o_up, o_dn, m_up, m_dn, r_up, r_dn, t_up, t_dn,
-    xs, act_s, pre_s, ys, gu, gd, parts, hparts, apack, wsend,
+    edisp, ebuf, xe, pa, epa, egu, egd,
+    xs, ys, gu, gd, parts, hparts, apack, wsend,
     m, r, ret, rbuf, hr, hret, rhot, apool, wrecv,
     load_s, disp_s, disp_r, y_s, y_r, y_f, h_s, h_r, hy_s, hy_r,
-    s1_s, s1_r, s1_l, s2_s, s2_m, s2_raw, s2_acc, s3_s, s3_r, s4_s, s4_r, s4_l, s5_s, s5_r, s5_f, s6_s, s6_r,
+    s1_s, s1_r, s1_l, s2_s, s2_m, s2_raw, s2_acc, s3_s, s3_r, s5_s, s5_r, s5_f, s6_s, s6_r,
     g_s, g_r, w_s, w_r, m_s, m_r, raw_s, raw_r, acc_s, acc_r, ret_s, ret_r,
     hp_s, hp_r, hret_s, hret_r, az_s, az_r, ax_s, ax_r, ac_s, ac_r,
+    ed_s, ed_r, ey_s, ey_r, ey_f, em_s, em_r, ef_s, eg_s,
 ):
     at = Place()
     y, x, z, c = at.y, at.x, at.z, at.c
@@ -258,11 +284,143 @@
         lax.fori_loop(0, 16, choose, 0)
 
     ring = ((o_up, m_up, r_up, t_up, 128), (o_dn, m_dn, r_dn, t_dn, 32))
-    for i, (o, mm, rr, t, n) in enumerate(ring):
+    full = ((uph, t_up, r_up, 64), (dnh, t_dn, r_dn, 16))
+
+    def hot_begin(i):
+        o, mm, rr, t, n = ring[i]
         send(o.at[rows(xo * 2 * n, n)], mm.at[0], s2_s.at[i, 0], s2_m.at[i, 0], at.at_x(xr))
         send(o.at[rows(xo * 2 * n + n, n)], mm.at[1], s2_s.at[i, 1], s2_m.at[i, 1], at.at_x(xl))
         send(o.at[rows(xr * 2 * n + n, n)], rr.at[0, pl.ds(n, n)], s2_s.at[i, 2], s2_raw.at[i, 0], at.at_x(xr))
         send(o.at[rows(xl * 2 * n, n)], rr.at[1, pl.ds(0, n)], s2_s.at[i, 3], s2_raw.at[i, 1], at.at_x(xl))
+
+    def hot_ring(i):
+        o, mm, rr, t, n = ring[i]
+        wait(mm.at[0], s2_m.at[i, 0])
+        mm[0] = mm[0] + o[rows(xr * 2 * n, n)]
+        send(mm.at[0], rr.at[0, pl.ds(0, n)], s2_s.at[i, 4], s2_acc.at[i, 0], at.at_x(xr))
+        wait(mm.at[1], s2_m.at[i, 1])
+        mm[1] = mm[1] + o[rows(xl * 2 * n + n, n)]
+        send(mm.at[1], rr.at[1, pl.ds(n, n)], s2_s.at[i, 5], s2_acc.at[i, 1], at.at_x(xl))
+
+    def hot_line(i):
+        o, mm, rr, t, n = ring[i]
+        for side, raw, acc in ((0, pl.ds(n, n), pl.ds(0, n)), (1, pl.ds(0, n), pl.ds(n, n))):
+            wait(rr.at[side, raw], s2_raw.at[i, side])
+            wait(rr.at[side, acc], s2_acc.at[i, side])
+        rr[0] = rr[0] + rr[1] + o[rows(x * 2 * n, 2 * n)]
+
+        @pl.when(z == 0)
+        def _():
+            send(rr.at[0], t.at[0], s3_s.at[i, 0], s3_r.at[i, 0], at.at_z(1))
+
+        @pl.when(z == 3)
+        def _():
+            send(rr.at[0], t.at[1], s3_s.at[i, 1], s3_r.at[i, 1], at.at_z(2))
+
+    def hot_up(i):
+        o, mm, rr, t, n = ring[i]
+
+        @pl.when(z > 0)
+        def _():
+            wait(t.at[0], s3_r.at[i, 0])
+
+            @pl.when(z < 3)
+            def _():
+                t[2] = t[0] + rr[0]
+                send(t.at[2], t.at[0], s3_s.at[i, 0], s3_r.at[i, 0], at.at_z(z + 1))
+
+    def hot_down(i):
+        o, mm, rr, t, n = ring[i]
+
+        @pl.when(z < 3)
+        def _():
+            wait(t.at[1], s3_r.at[i, 1])
+
+            @pl.when(z > 0)
+            def _():
+                t[3] = t[1] + rr[0]
+                send(t.at[3], t.at[1], s3_s.at[i, 1], s3_r.at[i, 1], at.at_z(z - 1))
+
+    def hot_near():
+        @pl.when(z < 2)
+        def _():
+            hot_up(0)
+            hot_up(1)
+
+        @pl.when(z >= 2)
+        def _():
+            hot_down(0)
+            hot_down(1)
+
+    def hot_far():
+        @pl.when(z < 2)
+        def _():
+            hot_down(0)
+            hot_down(1)
+
+        @pl.when(z >= 2)
+        def _():
+            hot_up(0)
+            hot_up(1)
+
+    def half_of(dst, w):
+        return lambda xx, b: dst.at[rows(c * 16 * w + xx * 4 * w + b * 2 * w, 2 * w)]
+
+    def quarter_of(dst, w, xx):
+        return dst.at[rows(c * 16 * w + xx * 4 * w, 4 * w)]
+
+    def hot_around(i):
+        dst, t, rr, w = full[i]
+        mine = rows(c * 16 * w + x * 4 * w, 4 * w)
+
+        @pl.when(z == 0)
+        def _():
+            dst[mine] = rr[0] + t[1]
+
+        @pl.when(z == 3)
+        def _():
+            dst[mine] = rr[0] + t[0]
+
+        @pl.when(jnp.logical_and(z > 0, z < 3))
+        def _():
+            dst[mine] = rr[0] + t[0] + t[1]
+
+        half = half_of(dst, w)
+        for b in range(2):
+            send(half(x, b), half(x, b), s5_s.at[i, b], s5_r.at[i, 0, b], at.at_x(xr))
+            send(half(x, 1 - b), half(x, 1 - b), s5_s.at[i, 2 + b], s5_r.at[i, 1, 1 - b], at.at_x(xl))
+        send(quarter_of(dst, w, x), quarter_of(dst, w, x), s6_s.at[i, 0], s6_r.at[i, 0], at.partner())
+
+    def hot_onward(i):
+        dst, t, rr, w = full[i]
+        half = half_of(dst, w)
+        wait(half(xl, 0), s5_r.at[i, 0, 0])
+        send(half(xl, 0), half(xl, 0), s5_s.at[i, 4], s5_f.at[i, 0], at.at_x(xr))
+        wait(half(xr, 1), s5_r.at[i, 1, 1])
+        send(half(xr, 1), half(xr, 1), s5_s.at[i, 5], s5_f.at[i, 1], at.at_x(xl))
+
+    def hot_partner(i):
+        dst, t, rr, w = full[i]
+        half = half_of(dst, w)
+        wait(half(xl, 1), s5_r.at[i, 0, 1])
+        wait(half(xr, 0), s5_r.at[i, 1, 0])
+        for k, xx in ((1, xl), (2, xr)):
+            send(quarter_of(dst, w, xx), quarter_of(dst, w, xx), s6_s.at[i, k], s6_r.at[i, k], at.partner())
+
+    def hot_last(i):
+        dst, t, rr, w = full[i]
+        half = half_of(dst, w)
+        wait(half(xo, 0), s5_f.at[i, 0])
+        wait(half(xo, 1), s5_f.at[i, 1])
+        send(quarter_of(dst, w, xo), quarter_of(dst, w, xo), s6_s.at[i, 3], s6_r.at[i, 3], at.partner())
+
+    def hot_arrived():
+        for i, (dst, t, rr, w) in enumerate(full):
+            for k in range(4):
+                wait(dst.at[pl.ds(0, 4 * w)], s6_r.at[i, k])
+
+    for i in range(2):
+        hot_begin(i)
 
     def slab(of_y, g):
         return buf.at[of_y, pl.ds(g * 8, 8)]
@@ -300,20 +458,30 @@
             preact += dot(xs[q, at_s], upv[q * 512 : (q + 1) * 512])
             dact += dot_nt(xs[4 + q, at_s], dnv[:, q * 512 : (q + 1) * 512])
         value, slope = gelu_pair(preact)
-        act_s[at_s] = value.astype(BF)
-        pre_s[at_s] = (dact * slope).astype(BF)
+        pa[1, at_s] = value.astype(BF)
+        pa[0, at_s] = (dact * slope).astype(BF)
+
+    inner = jnp.logical_or(z == 1, z == 2)
+
+    def share(i, s):
+        at_s = rows(s * 128, 128)
+
+        @pl.when(inner)
+        def _():
+            send(pa.at[:, at_s], epa.at[:, at_s], em_s, em_r.at[i], at.at_z(3 - z))
+
+    def share_outward(i, s):
+        at_s = rows(s * 128, 128)
+        wait(epa.at[:, at_s], em_r.at[i])
+
+        @pl.when(inner)
+        def _():
+            send(epa.at[:, at_s], epa.at[:, at_s], ef_s, em_r.at[i], at.at_z(3 * (z - 1)))
 
     for i in range(5):
         pass_on(i)
-
-    for i, (o, mm, rr, t, n) in enumerate(ring):
-        wait(mm.at[0], s2_m.at[i, 0])
-        mm[0] = mm[0] + o[rows(xr * 2 * n, n)]
-        send(mm.at[0], rr.at[0, pl.ds(0, n)], s2_s.at[i, 4], s2_acc.at[i, 0], at.at_x(xr))
-        wait(mm.at[1], s2_m.at[i, 1])
-        mm[1] = mm[1] + o[rows(xl * 2 * n + n, n)]
-        send(mm.at[1], rr.at[1, pl.ds(n, n)], s2_s.at[i, 5], s2_acc.at[i, 1], at.at_x(xl))
-
+    hot_ring(0)
+    hot_ring(1)
     for i in range(5, 8):
         pass_on(i)
 
@@ -322,39 +490,37 @@
     for k in range(1, 4):
         send(hbuf.at[y], hbuf.at[y], hy_s, hy_r, at.at_y((y + k) % 4))
 
-    for i in range(2):
-        forward(i)
+    forward(0)
+    forward(1)
+    pack_columns(hot, tokens, cot, gate_cols, ids_ref, slots_ref, edisp)
+    local(edisp.at[at.e], ebuf.at[y, at.me], ed_r)
+
+    def dispatch_columns(k, _):
+        p = (at.me + k) % 64
+        send(edisp.at[p % 32], ebuf.at[y, at.me], ed_s, ed_r, at.at_peer(p))
+        return 0
+
+    lax.fori_loop(1, 64, dispatch_columns, 0)
+    forward(2)
+    forward(3)
     wait(upv, load_s.at[0])
     wait(dnv, load_s.at[1])
     hidden(y)
-    for i in range(2, 4):
-        forward(i)
-
-    for i, (o, mm, rr, t, n) in enumerate(ring):
-        for side, raw, acc in ((0, pl.ds(n, n), pl.ds(0, n)), (1, pl.ds(0, n), pl.ds(n, n))):
-            wait(rr.at[side, raw], s2_raw.at[i, side])
-            wait(rr.at[side, acc], s2_acc.at[i, side])
-        rr[0] = rr[0] + rr[1] + o[rows(x * 2 * n, 2 * n)]
-        w = n // 2
-        for k in range(1, 4):
-            zz = (z + k) % 4
-            send(rr.at[0, rows(zz * w, w)], t.at[k - 1], s3_s.at[i, k - 1], s3_r.at[i, k - 1], at.at_z(zz))
-
+    share(0, y)
+    hot_line(0)
+    hot_line(1)
     for i in range(4, 8):
         forward(i)
-
-    full = ((uph, t_up, r_up, 64), (dnh, t_dn, r_dn, 16))
-    for i, (dst, t, rr, w) in enumerate(full):
-        for k in range(3):
-            wait(t.at[k], s3_r.at[i, k])
-        t[3] = t[0] + t[1] + t[2] + rr[0, rows(z * w, w)]
-        place = rows(c * 16 * w + x * 4 * w + z * w, w)
-        local(t.at[3], dst.at[place], s4_l.at[i])
-        for k in range(1, 4):
-            send(t.at[3], dst.at[place], s4_s.at[i, k - 1], s4_r.at[i, k - 1], at.at_z((z + k) % 4))
-
+    hot_near()
     hidden(yl)
+    share(1, yl)
+    wait(ebuf.at[y], ed_r)
+    send(ebuf.at[y], ebuf.at[y], ey_s, ey_r.at[0], at.at_y(yr))
+    send(ebuf.at[y], ebuf.at[y], ey_s, ey_r.at[1], at.at_y(yl))
+    share_outward(0, y)
     hidden(yr)
+    share(2, yr)
+    hot_far()
 
     wait(hbuf.at[pl.ds(0, 3)], hy_r)
     horder = order_matrix(8, 4)
@@ -378,32 +544,21 @@
 
     lax.fori_loop(1, 32, widths, 0)
 
-    def half_of(dst, w):
-        return lambda xx, b: dst.at[rows(c * 16 * w + xx * 4 * w + b * 2 * w, 2 * w)]
-
-    def quarter_of(dst, w, xx):
-        return dst.at[rows(c * 16 * w + xx * 4 * w, 4 * w)]
-
-    for i, (dst, t, rr, w) in enumerate(full):
-        wait(t.at[3], s4_l.at[i])
-        for k in range(3):
-            wait(t.at[3], s4_r.at[i, k])
-        half = half_of(dst, w)
-        for b in range(2):
-            send(half(x, b), half(x, b), s5_s.at[i, b], s5_r.at[i, 0, b], at.at_x(xr))
-            send(half(x, b), half(x, b), s5_s.at[i, 2 + b], s5_r.at[i, 1, b], at.at_x(xl))
-        send(quarter_of(dst, w, x), quarter_of(dst, w, x), s6_s.at[i, 0], s6_r.at[i, 0], at.partner())
-
+    hot_around(0)
+    hot_around(1)
+    share_outward(1, yl)
     for i in range(8):
         wait(slab(yo, groups[i]), y_f.at[i])
     hidden(yo)
+    share(3, yo)
+    share_outward(2, yr)
 
     local_at = rows(at.e * 64, 64)
 
     def gradients(q):
         here = rows(q * 512, 512)
-        gu[here] = dot_tn(xs[q], pre_s[...]).astype(BF)
-        gd[here] = dot_tn(xs[4 + q], act_s[...]).astype(BF)
+        gu[here] = dot_tn(xs[q], pa[0]).astype(BF)
+        gd[here] = dot_tn(xs[4 + q], pa[1]).astype(BF)
 
     def give_gradients(k, _, q):
         e = q * 8 + (at.e + k) % 8
@@ -416,8 +571,8 @@
         at_s = rows(s * 128, 128)
         for q in range(4):
             cols = slice(q * 512, (q + 1) * 512)
-            ys[q] = dot(act_s[at_s], dnv[:, cols]).astype(BF)
-            ys[4 + q] = dot_nt(pre_s[at_s], upv[cols, :]).astype(BF)
+            ys[q] = dot(pa[1, at_s], dnv[:, cols]).astype(BF)
+            ys[4 + q] = dot_nt(pa[0, at_s], upv[cols, :]).astype(BF)
 
         def unsort_rows(b, _):
             block = jnp.concatenate([ys[k, rows(b * 32, 32)] for k in range(8)], axis=0)
@@ -429,17 +584,27 @@
     def part(of_y, g):
         return parts.at[of_y, pl.ds(g * 8, 8)]
 
-    for k in (2, 1):
+    def direct(k):
         q = (z + k) % 4
-        gradients(q)
-        lax.fori_loop(0, 8, functools.partial(give_gradients, q=q), 0)
+        crosses = (z // 2) != (q // 2)
+
+        @pl.when(jnp.logical_not(jnp.logical_and(inner, crosses)))
+        def _():
+            gradients(q)
+            lax.fori_loop(0, 8, functools.partial(give_gradients, q=q), 0)
+
+    direct(2)
+    direct(1)
+    share_outward(3, yo)
     partial(yo)
     for i in range(4):
         send(part(yo, i), m.at[0, i], m_s, m_r.at[0, i], at.at_y(yr))
         send(part(yo, 4 + i), m.at[1, i], m_s, m_r.at[1, i], at.at_y(yl))
-    q = (z + 3) % 4
-    gradients(q)
-    lax.fori_loop(0, 8, functools.partial(give_gradients, q=q), 0)
+    wait(ebuf.at[yl], ey_r.at[0])
+    send(ebuf.at[yl, pl.ds(0, 32)], ebuf.at[yl, pl.ds(0, 32)], ey_s, ey_f.at[0], at.at_y(yr))
+    wait(ebuf.at[yr], ey_r.at[1])
+    send(ebuf.at[yr, pl.ds(32, 32)], ebuf.at[yr, pl.ds(32, 32)], ey_s, ey_f.at[1], at.at_y(yl))
+    direct(3)
     for s, to, first, side in ((yr, yr, 4, 0), (yl, yl, 0, 1)):
         partial(s)
         for i in range(4):
@@ -449,12 +614,8 @@
     local(gd.at[local_at], ogd.at[at.e], g_r.at[1])
     lax.fori_loop(1, 8, functools.partial(give_gradients, q=z), 0)
 
-    for i, (dst, t, rr, w) in enumerate(full):
-        half = half_of(dst, w)
-        wait(half(xl, 0), s5_r.at[i, 0, 0])
-        send(half(xl, 0), half(xl, 0), s5_s.at[i, 4], s5_f.at[i, 0], at.at_x(xr))
-        wait(half(xr, 1), s5_r.at[i, 1, 1])
-        send(half(xr, 1), half(xr, 1), s5_s.at[i, 5], s5_f.at[i, 1], at.at_x(xl))
+    hot_onward(0)
+    hot_onward(1)
 
     for i in range(4):
         wait(m.at[0, i], m_r.at[0, i])
@@ -463,22 +624,40 @@
         wait(m.at[1, i], m_r.at[1, i])
         m[1, i] = (m[1, i].astype(F32) + parts[yl, pl.ds(32 + i * 8, 8)].astype(F32)).astype(BF)
         send(m.at[1, i], r.at[1, 4 + i], acc_s, acc_r.at[1, i], at.at_y(yl))
+    wait(ebuf.at[yo, pl.ds(0, 32)], ey_f.at[0])
+    wait(ebuf.at[yo, pl.ds(32, 32)], ey_f.at[1])
+
+    def sort_columns(b, _):
+        s = b // 4
+        data = ebuf[s, pl.ds((b % 4) * 16, 16)].reshape(256, 128)
+        block = dot(order, data).astype(BF)
+        for k in range(8):
+            xe[k // 4, rows(b * 32, 32), (k % 4) * 128 : (k % 4 + 1) * 128] = block[k * 32 : (k + 1) * 32]
+        return 0
+
+    lax.fori_loop(0, 16, sort_columns, 0)
+    egu[...] = dot_tn(xe[0], epa[0]).astype(BF)
+    egd[...] = dot_tn(xe[1], epa[1]).astype(BF)
+    other_expert = (2 - z // 2) * 8 + at.e % 8
+    local(egu.at[rows((at.e % 8) * 64, 64)], ogu.at[other_expert], g_r.at[0])
+    local(egd.at[rows((at.e % 8) * 64, 64)], ogd.at[other_expert], g_r.at[1])
+
+    def give_other(k, _):
+        j = (at.e + k) % 8
+        to = (at.dp, z * 8 + j)
+        send(egu.at[rows(j * 64, 64)], ogu.at[other_expert], eg_s.at[0], g_r.at[0], to)
+        send(egd.at[rows(j * 64, 64)], ogd.at[other_expert], eg_s.at[1], g_r.at[1], to)
+        return 0
+
+    lax.fori_loop(1, 8, give_other, 0)
     partial(y)
 
-    for i, (dst, t, rr, w) in enumerate(full):
-        half = half_of(dst, w)
-        wait(half(xl, 1), s5_r.at[i, 0, 1])
-        wait(half(xr, 0), s5_r.at[i, 1, 0])
-        for k, xx in ((1, xl), (2, xr)):
-            send(quarter_of(dst, w, xx), quarter_of(dst, w, xx), s6_s.at[i, k], s6_r.at[i, k], at.partner())
-    for i, (dst, t, rr, w) in enumerate(full):
-        half = half_of(dst, w)
-        wait(half(xo, 0), s5_f.at[i, 0])
-        wait(half(xo, 1), s5_f.at[i, 1])
-        send(quarter_of(dst, w, xo), quarter_of(dst, w, xo), s6_s.at[i, 3], s6_r.at[i, 3], at.partner())
-    for i, (dst, t, rr, w) in enumerate(full):
-        for k in range(4):
-            wait(dst.at[pl.ds(0, 4 * w)], s6_r.at[i, k])
+    hot_partner(0)
+    hot_partner(1)
+    hot_last(0)
+    hot_last(1)
+
+    hot_arrived()
 
     preact = dot(hx[0], uph[0:512])
     dact = dot_nt(hx[4], dnh[:, 0:512])
@@ -565,16 +744,36 @@
     for i, (o, mm, rr, t, n) in enumerate(ring):
         for k in range(6):
             wait(mm.at[0], s2_s.at[i, k])
-        for k in range(3):
-            wait(t.at[0], s3_s.at[i, k])
-            wait(t.at[0], s4_s.at[i, k])
+
+        @pl.when(z < 3)
+        def _(i=i, t=t):
+            wait(t.at[0], s3_s.at[i, 0])
+
+        @pl.when(z > 0)
+        def _(i=i, t=t):
+            wait(t.at[0], s3_s.at[i, 1])
+
     for i, (dst, t, rr, w) in enumerate(full):
         for k in range(6):
             wait(dst.at[pl.ds(0, 2 * w)], s5_s.at[i, k])
         for k in range(4):
             wait(dst.at[pl.ds(0, 4 * w)], s6_s.at[i, k])
-    wait(gu.at[pl.ds(0, 31 * 64)], g_s.at[0])
-    wait(gd.at[pl.ds(0, 31 * 64)], g_s.at[1])
+    @pl.when(jnp.logical_not(inner))
+    def _():
+        wait(gu.at[pl.ds(0, 31 * 64)], g_s.at[0])
+        wait(gd.at[pl.ds(0, 31 * 64)], g_s.at[1])
+
+    @pl.when(inner)
+    def _():
+        wait(gu.at[pl.ds(0, 15 * 64)], g_s.at[0])
+        wait(gd.at[pl.ds(0, 15 * 64)], g_s.at[1])
+        wait(epa, em_s)
+        wait(epa, ef_s)
+
+    wait(egu.at[pl.ds(0, 7 * 64)], eg_s.at[0])
+    wait(egd.at[pl.ds(0, 7 * 64)], eg_s.at[1])
+    wait(ebuf.at[0, pl.ds(0, 63)], ed_s)
+    wait(ebuf.at[pl.ds(0, 3)], ey_s)
     wait(wsend.at[pl.ds(0, 31)], w_s)
     wait(m, m_s)
     wait(m, raw_s)
@@ -604,8 +803,10 @@
             vm(2048, 512), vm(512, 2048), vm(2048, 512), vm(512, 2048),
             vm(1024, 512), vm(256, 2048), vm(1024, 512), vm(256, 2048),
             vm(2, 128, 512), vm(2, 32, 2048), vm(2, 256, 512), vm(2, 64, 2048),
-            vm(4, 64, 512), vm(4, 16, 2048),
-            vm(8, 512, 512), vm(512, 512), vm(512, 512), vm(8, 128, 512),
+            vm(4, 256, 512), vm(4, 64, 2048),
+            vm(32, 16, 128), vm(4, 64, 16, 128), vm(2, 512, 512), vm(2, 512, 512), vm(2, 512, 512),
+            vm(512, 512), vm(512, 512),
+            vm(8, 512, 512), vm(8, 128, 512),
             vm(2048, 512), vm(2048, 512), vm(4, 64, 16, 512), vm(4, 2, 32, 512),
             vm(32, 1024), vm(32, 32, 128),
             vm(2, 4, 8, 16, 512), vm(2, 8, 8, 16, 512), vm(64, 16, 512), vm(64, 16, 512),
@@ -613,10 +814,11 @@
             DMA((2,)), DMA, DMA((8,)), DMA, DMA((2, 8)), DMA((8,)), DMA, DMA((2,)), DMA, DMA,
             DMA((2,)), DMA((2,)), DMA((2,)),
             DMA((2, 6)), DMA((2, 2)), DMA((2, 2)), DMA((2, 2)),
-            DMA((2, 3)), DMA((2, 3)), DMA((2, 3)), DMA((2, 3)), DMA((2,)),
+            DMA((2, 2)), DMA((2, 2)),
             DMA((2, 6)), DMA((2, 2, 2)), DMA((2, 2)), DMA((2, 4)), DMA((2, 4)),
             DMA((2,)), DMA((2,)), DMA, DMA, DMA, DMA((2, 4)), DMA, DMA((2, 4)), DMA, DMA((2, 4)), DMA, DMA,
             DMA, DMA((3,)), DMA, DMA((2,)), DMA, DMA((4,)), DMA, DMA((3,)), DMA, DMA,
+            DMA, DMA, DMA, DMA((2,)), DMA((2,)), DMA, DMA((4,)), DMA, DMA((2,)),
         ],
         compiler_params=pltpu.CompilerParams(
             collective_id=1, has_side_effects=True, vmem_limit_bytes=LIMIT

time: 215 us -> 207 us (0.963); the launches traced: 212 us -> 207 us
  Pallas kernels: 205 us -> 200 us
    pallas_call x1, Pallas kernels: 205 us -> 200 us  [layer(): pl.pallas_call(layer_kernel, out_shape=(sds((128, 2048)), sds((128, 2048)...]
where the time goes in v3:
time: 207 us
  Pallas kernels  200 us (97%)
  other arithmetic  5.39 us (3%)
    pallas_call x1, Pallas kernels, layer(): pl.pallas_call(layer_kernel, out_shape=(sds((128, 2048)), sds((128, 2048)...  200 us
    select_n x1, other arithmetic, on_device(): grad_down = jnp.where(is_hot, hdn[None], ogd)  4.73 us

profile of v3, /device:TPU:1, one launch (start us, length us, event | category | flops | bytes accessed | tf_op | source)
XLA Modules:
  0.0 207.3 jit_solution(11073734431701931174)
XLA Ops:
  0.6 0.7 broadcast_compare_fusion
  1.3 199.7 %layer.1 = (bf16[128,2048]{1,0:T(8,128)(2,1)}, bf16[128,2048]{1,0:T(8,128)(2,1)}, bf16[64,512]{1,0:T(8,128)(2,1)}, bf16[64,512]{1,0:T(8,128)(2,1)}, bf16[32,64,5...) custom-call(s32[32]{0:T(128)} %mask_ref.1, bf16[128,2048]{1,0:T(8,128)(2,1)} %tokens.1, bf16[128,2048]{1,0:T(8,128)(2,1)} %cot.1, ...), custom_call_target="tpu_custom_call" | custom-call | tf_op jit(solution)/shard_map/layer/pallas_call | solution.py:793
  201.0 0.0 copy-start.1
  201.0 0.0 copy-start
  201.0 4.7 %broadcast_select_fusion = (bf16[32,64,512]{2,1,0:T(8,128)(2,1)}, bf16[32,64,512]{2,1,0:T(8,128)(2,1)}) fusion(bf16[32,64,512]{2,1,0:T(8,128)(2,1)} %get-tuple-element.15, pred[32]{0:T(512)(128)(4,1)S(1)} %broadcast_compare_fusion, bf16[64,512]{1,0:T(8,128)(2,1)} %get-tuple-element.14, bf16[32,64,512]{2,1,0:T(8,128)(2,1)} %get-tuple-element.13, ...), kind=kLoop, calls=%fused_computation | loop fusion | flops 2097152 | bytes 8519712 | tf_op jit(solution)/shard_map/jit(_where)/select_n | solution.py:836
  205.7 0.0 copy-done.1
  205.7 0.8 copy.14
  206.5 0.0 copy-done
  206.5 0.8 copy.15
Async XLA Ops:
  201.0 4.8 %copy-start.1 = (bf16[128,2048]{1,0:T(8,128)(2,1)S(1)}, bf16[128,2048]{1,0:T(8,128)(2,1)}, u32[]{:S(2)}) copy-start(bf16[128,2048]{1,0:T(8,128)(2,1)} %get-tuple-element.22) | copy-start | bytes 1572868
  201.0 5.5 %copy-start = (bf16[128,2048]{1,0:T(8,128)(2,1)S(1)}, bf16[128,2048]{1,0:T(8,128)(2,1)}, u32[]{:S(2)}) copy-start(bf16[128,2048]{1,0:T(8,128)(2,1)} %get-tuple-element.23) | copy-start | bytes 1572868

commit v4 on v3

--- a/solution.py
+++ b/solution.py
@@ -179,7 +179,7 @@
         edisp[q * 8 : (q + 1) * 8] = out.astype(BF).reshape(8, 16, 128)
 
 
-def combine_rows(hot, rbuf, rhot, gate_cols, id_cols, slot_cols, out_ref, back_ref):
+def make_picks(hot, id_cols, slot_cols, picks, hpicks):
     r = iota((128, 1024), 1)
     code = ((r // 16) % 32) * CAP + (r // 4) % 2
     is_back = (r // 8) % 2
@@ -193,21 +193,26 @@
         normal, special = places_of(id_cols[k], slot_cols[k], hot)
         sel.append(code == normal)
         hsel.append(hcode == special)
+    sel.append(jnp.logical_or(sel[0], sel[1]))
+    hsel.append(jnp.logical_or(hsel[0], hsel[1]))
+    for q in range(4):
+        for k, kind in ((0, 0), (1, 0), (2, 1)):
+            picks[q * 3 + k] = ones_where(
+                jnp.logical_and(jnp.logical_and(sel[k], quarter == q), is_back == kind)
+            )
+            hpicks[q * 3 + k] = ones_where(
+                jnp.logical_and(jnp.logical_and(hsel[k], hquarter == q), h_is_back == kind)
+            )
+
+
+def combine_rows(picks, hpicks, rbuf, rhot, gate_cols, out_ref, back_ref):
     data = rbuf[...].reshape(1024, 512)
     hdata = rhot[...].reshape(64, 512)
-
-    def pick(s, hs, q, kind):
-        m = ones_where(jnp.logical_and(jnp.logical_and(s, quarter == q), is_back == kind))
-        hm = ones_where(jnp.logical_and(jnp.logical_and(hs, hquarter == q), h_is_back == kind))
-        return dot(m, data) + dot(hm, hdata)
-
-    either = jnp.logical_or(sel[0], sel[1])
-    heither = jnp.logical_or(hsel[0], hsel[1])
     for q in range(4):
         cols = slice(q * 512, (q + 1) * 512)
-        out = gate_cols[0] * pick(sel[0], hsel[0], q, 0) + gate_cols[1] * pick(sel[1], hsel[1], q, 0)
-        out_ref[:, cols] = out.astype(BF)
-        back_ref[:, cols] = pick(either, heither, q, 1).astype(BF)
+        got = [dot(picks[q * 3 + k], data) + dot(hpicks[q * 3 + k], hdata) for k in range(3)]
+        out_ref[:, cols] = (gate_cols[0] * got[0] + gate_cols[1] * got[1]).astype(BF)
+        back_ref[:, cols] = got[2].astype(BF)
 
 
 def layer_kernel(
@@ -215,7 +220,7 @@
     out_ref, back_ref, hup_ref, hdn_ref, ogu, ogd,
     disp, hrow, buf, hbuf, upv, dnv, uph, dnh,
     p_up, p_dn, o_up, o_dn, m_up, m_dn, r_up, r_dn, t_up, t_dn,
-    edisp, ebuf, xe, pa, epa, egu, egd,
+    edisp, ebuf, xe, pa, epa, egu, egd, picks, hpicks,
     xs, ys, gu, gd, parts, hparts, apack, wsend,
     m, r, ret, rbuf, hr, hret, rhot, apool, wrecv,
     load_s, disp_s, disp_r, y_s, y_r, y_f, h_s, h_r, hy_s, hy_r,
@@ -600,6 +605,8 @@
     for i in range(4):
         send(part(yo, i), m.at[0, i], m_s, m_r.at[0, i], at.at_y(yr))
         send(part(yo, 4 + i), m.at[1, i], m_s, m_r.at[1, i], at.at_y(yl))
+    hot_onward(0)
+    hot_onward(1)
     wait(ebuf.at[yl], ey_r.at[0])
     send(ebuf.at[yl, pl.ds(0, 32)], ebuf.at[yl, pl.ds(0, 32)], ey_s, ey_f.at[0], at.at_y(yr))
     wait(ebuf.at[yr], ey_r.at[1])
@@ -614,8 +621,6 @@
     local(gd.at[local_at], ogd.at[at.e], g_r.at[1])
     lax.fori_loop(1, 8, functools.partial(give_gradients, q=z), 0)
 
-    hot_onward(0)
-    hot_onward(1)
 
     for i in range(4):
         wait(m.at[0, i], m_r.at[0, i])
@@ -714,6 +719,9 @@
     ).astype(BF)
     local(hret.at[at.h], rhot.at[at.h], hret_r.at[0])
     send(hret.at[1 - at.h], rhot.at[at.h], hret_s, hret_r.at[1], at.at_peer((at.me + 32) % 64))
+    id_cols = [to_column(ids_ref[k : k + 1, :]) for k in range(2)]
+    slot_cols = [to_column(slots_ref[k : k + 1, :]) for k in range(2)]
+    make_picks(hot, id_cols, slot_cols, picks, hpicks)
     for k in range(3):
         wait(apool.at[:, 0, 0], ax_r.at[k])
     send(apool.at[:, :, c], apool.at[:, :, c], ac_s, ac_r, at.partner())
@@ -728,9 +736,7 @@
     wait(rbuf, ret_r)
     wait(rhot.at[0], hret_r.at[0])
     wait(rhot.at[0], hret_r.at[1])
-    id_cols = [to_column(ids_ref[k : k + 1, :]) for k in range(2)]
-    slot_cols = [to_column(slots_ref[k : k + 1, :]) for k in range(2)]
-    combine_rows(hot, rbuf, rhot, gate_cols, id_cols, slot_cols, out_ref, back_ref)
+    combine_rows(picks, hpicks, rbuf, rhot, gate_cols, out_ref, back_ref)
 
     wait(ogu, g_r.at[0])
     wait(ogd, g_r.at[1])
@@ -805,7 +811,7 @@
             vm(2, 128, 512), vm(2, 32, 2048), vm(2, 256, 512), vm(2, 64, 2048),
             vm(4, 256, 512), vm(4, 64, 2048),
             vm(32, 16, 128), vm(4, 64, 16, 128), vm(2, 512, 512), vm(2, 512, 512), vm(2, 512, 512),
-            vm(512, 512), vm(512, 512),
+            vm(512, 512), vm(512, 512), vm(12, 128, 1024), vm(12, 128, 64),
             vm(8, 512, 512), vm(8, 128, 512),
             vm(2048, 512), vm(2048, 512), vm(4, 64, 16, 512), vm(4, 2, 32, 512),
             vm(32, 1024), vm(32, 32, 128),

time: 207 us -> 208 us (level)
  no operation moved by 1% of the time
where the time goes in v4:
time: 208 us
  Pallas kernels  201 us (97%)
  other arithmetic  5.39 us (3%)
    pallas_call x1, Pallas kernels, layer(): pl.pallas_call(layer_kernel, out_shape=(sds((128, 2048)), sds((128, 2048)...  201 us
    select_n x1, other arithmetic, on_device(): grad_down = jnp.where(is_hot, hdn[None], ogd)  4.73 us

profile of v4, /device:TPU:1, one launch (start us, length us, event | category | flops | bytes accessed | tf_op | source)
XLA Modules:
  0.0 208.2 jit_solution(421181263627058767)
XLA Ops:
  0.6 0.7 broadcast_compare_fusion
  1.3 200.6 %layer.1 = (bf16[128,2048]{1,0:T(8,128)(2,1)}, bf16[128,2048]{1,0:T(8,128)(2,1)}, bf16[64,512]{1,0:T(8,128)(2,1)}, bf16[64,512]{1,0:T(8,128)(2,1)}, bf16[32,64,5...) custom-call(s32[32]{0:T(128)} %mask_ref.1, bf16[128,2048]{1,0:T(8,128)(2,1)} %tokens.1, bf16[128,2048]{1,0:T(8,128)(2,1)} %cot.1, ...), custom_call_target="tpu_custom_call" | custom-call | tf_op jit(solution)/shard_map/layer/pallas_call | solution.py:799
  201.9 0.0 copy-start.1
  201.9 0.0 copy-start
  201.9 4.7 %broadcast_select_fusion = (bf16[32,64,512]{2,1,0:T(8,128)(2,1)}, bf16[32,64,512]{2,1,0:T(8,128)(2,1)}) fusion(bf16[32,64,512]{2,1,0:T(8,128)(2,1)} %get-tuple-element.15, pred[32]{0:T(512)(128)(4,1)S(1)} %broadcast_compare_fusion, bf16[64,512]{1,0:T(8,128)(2,1)} %get-tuple-element.14, bf16[32,64,512]{2,1,0:T(8,128)(2,1)} %get-tuple-element.13, ...), kind=kLoop, calls=%fused_computation | loop fusion | flops 2097152 | bytes 8519712 | tf_op jit(solution)/shard_map/jit(_where)/select_n | solution.py:842
  206.6 0.0 copy-done.1
  206.6 0.8 copy.14
  207.4 0.0 copy-done
  207.4 0.8 copy.15
Async XLA Ops:
  201.9 4.8 %copy-start.1 = (bf16[128,2048]{1,0:T(8,128)(2,1)S(1)}, bf16[128,2048]{1,0:T(8,128)(2,1)}, u32[]{:S(2)}) copy-start(bf16[128,2048]{1,0:T(8,128)(2,1)} %get-tuple-element.22) | copy-start | bytes 1572868
  201.9 5.5 %copy-start = (bf16[128,2048]{1,0:T(8,128)(2,1)S(1)}, bf16[128,2048]{1,0:T(8,128)(2,1)}, u32[]{:S(2)}) copy-start(bf16[128,2048]{1,0:T(8,128)(2,1)} %get-tuple-element.23) | copy-start | bytes 1572868
